TPU v7x, 32 devices: a whole 2x2x4 slice. The times are simulated.
32 devices in a mesh: ctx: 16 (over z, x, core), fsdp: 2 (over y).
Axes of the slice: x: 2, y: 2, z: 4, core: 2. Of those that a mesh axis runs over, the one named last changes fastest.
Arguments:
- tokens: bfloat16 [2, 4096, 1024], P('fsdp', 'ctx'), may hold values from -6 to 6
- cotangent: bfloat16 [2, 4096, 1024], P('fsdp', 'ctx'), may hold values from -6 to 6
- first_gain: bfloat16 [1024], P('fsdp'), may hold values from 0.5 to 1.5
- first_shift: bfloat16 [1024], P('fsdp'), may hold values from -1.5 to 1.5
- second_gain: bfloat16 [1024], P('fsdp'), may hold values from 0.5 to 1.5
- second_shift: bfloat16 [1024], P('fsdp'), may hold values from -1.5 to 1.5
- joint_weight: bfloat16 [1024, 3072], P('fsdp'), may hold values from -0.1875 to 0.1875
- joint_bias: bfloat16 [3072], P('fsdp'), may hold values from -1.5 to 1.5
- dense_weight: bfloat16 [1024, 1024], P('fsdp'), may hold values from -6 to 6
- dense_bias: bfloat16 [1024], P('fsdp'), may hold values from -1.5 to 1.5
- expand_weight: bfloat16 [1024, 4096], P('fsdp'), may hold values from -0.1875 to 0.1875
- expand_bias: bfloat16 [4096], P('fsdp'), may hold values from -1.5 to 1.5
- shrink_weight: bfloat16 [4096, 1024], P('fsdp'), may hold values from -0.09375 to 0.09375
- shrink_bias: bfloat16 [1024], P('fsdp'), may hold values from -1.5 to 1.5
- block_order: int32 [32], replicated, may hold values from 0 to 31, as said below
Outputs:
- layer_output: bfloat16 [2, 4096, 1024], P('fsdp', 'ctx')
- tokens_grad: bfloat16 [2, 4096, 1024], P('fsdp', 'ctx')
- first_gain_grad: float32 [1024], P('fsdp')
- first_shift_grad: float32 [1024], P('fsdp')
- second_gain_grad: float32 [1024], P('fsdp')
- second_shift_grad: float32 [1024], P('fsdp')
- joint_weight_grad: float32 [1024, 3072], P('fsdp')
- joint_bias_grad: float32 [3072], P('fsdp')
- dense_weight_grad: float32 [1024, 1024], P('fsdp')
- dense_bias_grad: float32 [1024], P('fsdp')
- expand_weight_grad: float32 [1024, 4096], P('fsdp')
- expand_bias_grad: float32 [4096], P('fsdp')
- shrink_weight_grad: float32 [4096, 1024], P('fsdp')
- shrink_bias_grad: float32 [1024], P('fsdp')
Inputs may be any that keep to these rules, and one draw needn't show every extreme that they name: `block_order`: slots 2i and 2i + 1 hold two blocks b and 31 - b in either order; every block of 0 to 31 is held once.
All inputs are finite; a program needn't handle non-finite values.
Results may differ from a plain program's by a relative error of at most 0.018.
Values may be sent and summed in bfloat16 or wider, within the bound.
No kernel may reach another device: no remote copies, remote signals or barrier semaphores. Data moves between devices by JAX's collectives and lax.ppermute only.
A program may use at most 256 MiB of HBM per device.

v0:
```python
import jax
import jax.numpy as jnp
from jax import lax
from jax.sharding import PartitionSpec as P

HEADS = 16
ROT = 16


epsilon = 1e-05
negative = -1e30


def normalize(values, gain, shift):
    center = values - jnp.mean(values, -1, keepdims=True)
    spread = jnp.mean(center * center, -1, keepdims=True)
    return center * lax.rsqrt(spread + epsilon) * gain + shift


def turn_tables(positions):
    inverse = jnp.power(10000.0, -2.0 * jnp.arange(ROT // 2, dtype=jnp.float32) / ROT)
    angles = positions.astype(jnp.float32)[:, None] * inverse[None, :]
    angles = jnp.concatenate([angles, angles], -1)[:, None, :]
    return (jnp.cos(angles), jnp.sin(angles))


def rotate(values, cosine, sine):
    half = ROT // 2
    front = values[..., :ROT]
    turned = jnp.concatenate([-front[..., half:], front[..., :half]], -1)
    return jnp.concatenate([front * cosine + turned * sine, values[..., ROT:]], -1)


def contract(left, right, left_dim, right_dim):
    return lax.dot_general(
        left, right, (((left_dim,), (right_dim,)), ((), ())), preferred_element_type=jnp.float32
    )


def shards(
    tokens,
    cotangent,
    first_gain,
    first_shift,
    second_gain,
    second_shift,
    joint_weight,
    joint_bias,
    dense_weight,
    dense_bias,
    expand_weight,
    expand_bias,
    shrink_weight,
    shrink_bias,
    block_order,
):
    rows = tokens.shape[1]
    width = tokens.shape[2]
    head_dim = width // HEADS
    scale = head_dim ** (-0.5)
    groups = lax.axis_size("ctx")
    half_rows = rows // 2
    (
        gain_one,
        shift_one,
        gain_two,
        shift_two,
        joint_full,
        joint_shift,
        dense_full,
        dense_shift,
        expand_full,
        expand_shift,
        shrink_full,
        shrink_shift,
    ) = (
        lax.all_gather(first_gain, "fsdp", axis=0, tiled=True),
        lax.all_gather(first_shift, "fsdp", axis=0, tiled=True),
        lax.all_gather(second_gain, "fsdp", axis=0, tiled=True),
        lax.all_gather(second_shift, "fsdp", axis=0, tiled=True),
        lax.all_gather(joint_weight, "fsdp", axis=0, tiled=True),
        lax.all_gather(joint_bias, "fsdp", axis=0, tiled=True),
        lax.all_gather(dense_weight, "fsdp", axis=0, tiled=True),
        lax.all_gather(dense_bias, "fsdp", axis=0, tiled=True),
        lax.all_gather(expand_weight, "fsdp", axis=0, tiled=True),
        lax.all_gather(expand_bias, "fsdp", axis=0, tiled=True),
        lax.all_gather(shrink_weight, "fsdp", axis=0, tiled=True),
        lax.all_gather(shrink_bias, "fsdp", axis=0, tiled=True),
    )
    gain_one = gain_one.astype(jnp.float32)
    shift_one = shift_one.astype(jnp.float32)
    gain_two = gain_two.astype(jnp.float32)
    shift_two = shift_two.astype(jnp.float32)
    all_positions = (
        block_order[:, None] * half_rows + jnp.arange(half_rows, dtype=jnp.int32)[None, :]
    ).reshape(rows * groups)
    positions = lax.dynamic_slice_in_dim(all_positions, lax.axis_index("ctx") * rows, rows)
    cosine, sine = turn_tables(positions)
    visible = positions[:, None] >= all_positions[None, :]
    inputs = tokens[0].astype(jnp.float32)
    normed_one = normalize(inputs, gain_one, shift_one).astype(jnp.bfloat16)
    normed_two = normalize(inputs, gain_two, shift_two).astype(jnp.bfloat16)
    joint = jnp.dot(
        normed_one, joint_full, preferred_element_type=jnp.float32
    ) + joint_shift.astype(jnp.float32)
    queries = (
        rotate(joint[:, :width].reshape(rows, HEADS, head_dim), cosine, sine)
        .reshape(rows, width)
        .astype(jnp.bfloat16)
    )
    key_rows = (
        rotate(joint[:, width : 2 * width].reshape(rows, HEADS, head_dim), cosine, sine)
        .reshape(rows, width)
        .astype(jnp.bfloat16)
    )
    value_rows = joint[:, 2 * width :].astype(jnp.bfloat16)
    all_keys, all_values = (
        lax.all_gather(key_rows, "ctx", axis=0, tiled=True),
        lax.all_gather(value_rows, "ctx", axis=0, tiled=True),
    )

    def head_scores(head, key_source):
        query = lax.dynamic_slice_in_dim(queries, head * head_dim, head_dim, 1)
        key_cols = lax.dynamic_slice_in_dim(key_source, head * head_dim, head_dim, 1)
        scores = contract(query, key_cols, 1, 1) * scale
        return (query, key_cols, jnp.where(visible, scores, negative))

    def head_forward(head):
        query, key_cols, scores = head_scores(head, all_keys)
        top = jnp.max(scores, -1, keepdims=True)
        total = jnp.sum(jnp.exp(scores - top), -1, keepdims=True)
        log_total = top + jnp.log(total)
        weights = jnp.exp(scores - log_total).astype(jnp.bfloat16)
        value_cols = lax.dynamic_slice_in_dim(all_values, head * head_dim, head_dim, 1)
        return (jnp.dot(weights, value_cols, preferred_element_type=jnp.float32), log_total[:, 0])

    mixed, log_totals = lax.map(head_forward, jnp.arange(HEADS))
    attended = jnp.transpose(mixed, (1, 0, 2)).reshape(rows, width).astype(jnp.bfloat16)
    expanded = jnp.dot(
        normed_two, expand_full, preferred_element_type=jnp.float32
    ) + expand_shift.astype(jnp.float32)
    activated = jax.nn.gelu(expanded, approximate=False).astype(jnp.bfloat16)
    output = (
        inputs
        + jnp.dot(attended, dense_full, preferred_element_type=jnp.float32)
        + dense_shift.astype(jnp.float32)
    )
    output = (
        output
        + jnp.dot(activated, shrink_full, preferred_element_type=jnp.float32)
        + shrink_shift.astype(jnp.float32)
    )
    upstream = cotangent[0]
    upstream_float = upstream.astype(jnp.float32)
    column_sum = jnp.sum(upstream_float, 0)
    dense_grad = contract(attended, upstream, 0, 0)
    shrink_grad = contract(activated, upstream, 0, 0)
    act_grad = contract(upstream, shrink_full, 1, 1)
    _, gelu_pull = jax.vjp(lambda value: jax.nn.gelu(value, approximate=False), expanded)
    expand_delta = gelu_pull(act_grad)[0].astype(jnp.bfloat16)
    expand_grad = contract(normed_two, expand_delta, 0, 0)
    expand_bias_grad = jnp.sum(expand_delta.astype(jnp.float32), 0)
    normed_two_grad = contract(expand_delta, expand_full, 1, 1)
    _, pull_two = jax.vjp(normalize, inputs, gain_two, shift_two)
    input_two, gain_two_grad, shift_two_grad = pull_two(normed_two_grad)
    attended_grad = contract(upstream, dense_full, 1, 1).astype(jnp.bfloat16)
    key_source, value_source = (all_keys, all_values)

    def head_backward(items):
        head, log_total = items
        query, key_cols, scores = head_scores(head, key_source)
        probs = jnp.exp(scores - log_total[:, None])
        value_cols = lax.dynamic_slice_in_dim(value_source, head * head_dim, head_dim, 1)
        out_grad = lax.dynamic_slice_in_dim(attended_grad, head * head_dim, head_dim, 1)
        prob_grad = contract(out_grad, value_cols, 1, 1)
        inner = jnp.sum(probs * prob_grad, -1, keepdims=True)
        score_grad = (probs * (prob_grad - inner)).astype(jnp.bfloat16)
        query_grad = jnp.dot(score_grad, key_cols, preferred_element_type=jnp.float32) * scale
        key_grad = contract(score_grad, query, 0, 0) * scale
        value_grad = contract(probs.astype(jnp.bfloat16), out_grad, 0, 0)
        return (query_grad, key_grad, value_grad)

    query_grads, key_grads, value_grads = lax.map(head_backward, (jnp.arange(HEADS), log_totals))
    key_sums, value_sums = (
        lax.psum_scatter(
            key_grads.astype(jnp.bfloat16), "ctx", scatter_dimension=1, tiled=True
        ).astype(jnp.float32),
        lax.psum_scatter(
            value_grads.astype(jnp.bfloat16), "ctx", scatter_dimension=1, tiled=True
        ).astype(jnp.float32),
    )
    query_back = rotate(jnp.transpose(query_grads, (1, 0, 2)), cosine, -sine).reshape(rows, width)
    key_back = rotate(jnp.transpose(key_sums, (1, 0, 2)), cosine, -sine).reshape(rows, width)
    value_back = jnp.transpose(value_sums, (1, 0, 2)).reshape(rows, width)
    joint_delta = jnp.concatenate([query_back, key_back, value_back], 1).astype(jnp.bfloat16)
    joint_grad = contract(normed_one, joint_delta, 0, 0)
    joint_bias_grad = jnp.sum(joint_delta.astype(jnp.float32), 0)
    normed_one_grad = contract(joint_delta, joint_full, 1, 1)
    _, pull_one = jax.vjp(normalize, inputs, gain_one, shift_one)
    input_one, gain_one_grad, shift_one_grad = pull_one(normed_one_grad)
    tokens_grad = (upstream_float + input_one + input_two).astype(jnp.bfloat16)
    (
        gain_one_part,
        shift_one_part,
        gain_two_part,
        shift_two_part,
        joint_part,
        joint_bias_part,
        dense_part,
        column_part,
        expand_part,
        expand_bias_part,
        shrink_part,
    ) = (
        lax.psum_scatter(
            gain_one_grad.astype(jnp.bfloat16), "fsdp", scatter_dimension=0, tiled=True
        ).astype(jnp.float32),
        lax.psum_scatter(
            shift_one_grad.astype(jnp.bfloat16), "fsdp", scatter_dimension=0, tiled=True
        ).astype(jnp.float32),
        lax.psum_scatter(
            gain_two_grad.astype(jnp.bfloat16), "fsdp", scatter_dimension=0, tiled=True
        ).astype(jnp.float32),
        lax.psum_scatter(
            shift_two_grad.astype(jnp.bfloat16), "fsdp", scatter_dimension=0, tiled=True
        ).astype(jnp.float32),
        lax.psum_scatter(
            joint_grad.astype(jnp.bfloat16), "fsdp", scatter_dimension=0, tiled=True
        ).astype(jnp.float32),
        lax.psum_scatter(
            joint_bias_grad.astype(jnp.bfloat16), "fsdp", scatter_dimension=0, tiled=True
        ).astype(jnp.float32),
        lax.psum_scatter(
            dense_grad.astype(jnp.bfloat16), "fsdp", scatter_dimension=0, tiled=True
        ).astype(jnp.float32),
        lax.psum_scatter(
            column_sum.astype(jnp.bfloat16), "fsdp", scatter_dimension=0, tiled=True
        ).astype(jnp.float32),
        lax.psum_scatter(
            expand_grad.astype(jnp.bfloat16), "fsdp", scatter_dimension=0, tiled=True
        ).astype(jnp.float32),
        lax.psum_scatter(
            expand_bias_grad.astype(jnp.bfloat16), "fsdp", scatter_dimension=0, tiled=True
        ).astype(jnp.float32),
        lax.psum_scatter(
            shrink_grad.astype(jnp.bfloat16), "fsdp", scatter_dimension=0, tiled=True
        ).astype(jnp.float32),
    )
    (
        gain_one_total,
        shift_one_total,
        gain_two_total,
        shift_two_total,
        joint_total,
        joint_bias_total,
        dense_total,
        column_total,
        expand_total,
        expand_bias_total,
        shrink_total,
    ) = (
        lax.psum(gain_one_part.astype(jnp.bfloat16), "ctx").astype(jnp.float32),
        lax.psum(shift_one_part.astype(jnp.bfloat16), "ctx").astype(jnp.float32),
        lax.psum(gain_two_part.astype(jnp.bfloat16), "ctx").astype(jnp.float32),
        lax.psum(shift_two_part.astype(jnp.bfloat16), "ctx").astype(jnp.float32),
        lax.psum(joint_part.astype(jnp.bfloat16), "ctx").astype(jnp.float32),
        lax.psum(joint_bias_part.astype(jnp.bfloat16), "ctx").astype(jnp.float32),
        lax.psum(dense_part.astype(jnp.bfloat16), "ctx").astype(jnp.float32),
        lax.psum(column_part.astype(jnp.bfloat16), "ctx").astype(jnp.float32),
        lax.psum(expand_part.astype(jnp.bfloat16), "ctx").astype(jnp.float32),
        lax.psum(expand_bias_part.astype(jnp.bfloat16), "ctx").astype(jnp.float32),
        lax.psum(shrink_part.astype(jnp.bfloat16), "ctx").astype(jnp.float32),
    )
    return (
        output.astype(jnp.bfloat16)[None],
        tokens_grad[None],
        gain_one_total,
        shift_one_total,
        gain_two_total,
        shift_two_total,
        joint_total,
        joint_bias_total,
        dense_total,
        column_total,
        expand_total,
        expand_bias_total,
        shrink_total,
        column_total,
    )


def solution(mesh):
    return jax.shard_map(
        shards,
        mesh=mesh,
        in_specs=(
            P("fsdp", "ctx", None),
            P("fsdp", "ctx", None),
            P("fsdp"),
            P("fsdp"),
            P("fsdp"),
            P("fsdp"),
            P("fsdp", None),
            P("fsdp"),
            P("fsdp", None),
            P("fsdp"),
            P("fsdp", None),
            P("fsdp"),
            P("fsdp", None),
            P("fsdp"),
            P(),
        ),
        out_specs=(
            P("fsdp", "ctx", None),
            P("fsdp", "ctx", None),
            P("fsdp"),
            P("fsdp"),
            P("fsdp"),
            P("fsdp"),
            P("fsdp", None),
            P("fsdp"),
            P("fsdp", None),
            P("fsdp"),
            P("fsdp", None),
            P("fsdp"),
            P("fsdp", None),
            P("fsdp"),
        ),
        check_vma=False,
    )
```

profile of v0, /device:TPU:0, one launch (start us, length us, event | category | flops | bytes accessed | tf_op | source)
XLA Modules:
  0.0 1401.0 jit_solution(16956023106531051924)
XLA Ops:
  9.3 5.3 all-gather
  14.5 4.3 all-gather.1
  18.9 4.4 all-gather.2
  24.2 68.5 %all-gather.14.cloned.1.call-done = bf16[1024,3072]{1,0:T(8,128)(2,1)} async-done(((bf16[512,3072]{1,0:T(8,128)(2,1)}), bf16[1024,3072]{1,0:T(8,128)(2,1)}) %all-gather.14.cloned.1.call-update) | async-done | bytes 6291472 | tf_op jit(solution)/shard_map/all_gather | solution.py:81
  92.7 4.7 convolution_add_fusion.1
  108.9 18.5 %all-gather.20.cloned.1.call-done = bf16[1024,1024]{1,0:T(8,128)(2,1)} async-done(((bf16[512,1024]{1,0:T(8,128)(2,1)}), bf16[1024,1024]{1,0:T(8,128)(2,1)}) %all-gather.20.cloned.1.call-update) | async-done | bytes 2097168 | tf_op jit(solution)/shard_map/all_gather | solution.py:83
  130.0 78.3 %all-gather.16.cloned.1.call-done = bf16[4096,1024]{0,1:T(8,128)(2,1)} async-done(((bf16[256,1024]{0,1:T(8,128)(2,1)}), bf16[4096,1024]{0,1:T(8,128)(2,1)}) %all-gather.16.cloned.1.call-update) | async-done | bytes 8388624 | tf_op jit(solution)/shard_map/all_gather | solution.py:118
  208.3 12.0 copy.46
  220.3 63.7 %all-gather.18.cloned.1.call-done = bf16[4096,1024]{1,0:T(8,128)(2,1)} async-done(((bf16[256,1024]{1,0:T(8,128)(2,1)}), bf16[4096,1024]{1,0:T(8,128)(2,1)}) %all-gather.18.cloned.1.call-update) | async-done | bytes 8388624 | tf_op jit(solution)/shard_map/all_gather | solution.py:119
  284.0 113.4 %while.30 = (s32[]{:T(128)}, bf16[16,256,64]{1,2,0:T(8,128)(2,1)S(1)}, f32[16,256]{1,0:T(8,128)S(1)}, s32[16]{0:T(128)S(1)}, bf16[256,1024]{1,0:T(8,128)(2,1)S(1...) while((s32[]{:T(128)}, ...), condition=%wide.region_5.6_spmd.clone.clone, body=%wide.region_2.5_spmd.clone.sunk.clone | while | flops 276823808 | bytes 14839463 | solution.py:137
  397.4 210.9 %while.31 = (s32[]{:T(128)}, f32[16,256,64]{1,2,0:T(8,128)}, bf16[16,4096,64]{1,2,0:T(8,128)(2,1)}, bf16[16,4096,64]{1,2,0:T(8,128)(2,1)}, s32[16]{0:T(128)S(1)}...) while((s32[]{:T(128)}, f32[16,256,64]{1,2,0:T(8,128)}, ...), condition=%wide.region_8.9_spmd.clone.clone, body=%wide.region_6.0_spmd.clone.sunk.clone | while | flops 681852672 | bytes 37054152 | solution.py:183
  407.7 3.3 fusion.162
  420.9 3.2 fusion.162
  434.1 3.2 fusion.162
  473.5 3.2 fusion.162
  486.7 3.2 fusion.162
  499.8 3.2 fusion.162
  526.2 3.2 fusion.162
  539.3 3.2 fusion.162
  552.4 3.2 fusion.162
  565.6 3.2 fusion.162
  578.8 3.2 fusion.162
  591.9 3.2 fusion.162
  605.1 3.2 fusion.162
  609.1 4.3 all-gather.4
  613.5 4.3 all-gather.5
  617.8 4.7 all_gather.53
  622.6 16.6 %multiply_convert_fusion.1 = (bf16[256,4096]{1,0:T(8,128)(2,1)}, f32[256,4096]{1,0:T(8,128)}, f32[256,4096]{1,0:T(8,128)}) fusion(f32[4096]{0:T(1024)S(1)} %convert_element_type.195, bf16[1024,4096]{1,0:T(8,128)(2,1)} %all-gather.22.cloned.1.call-done, bf16[1,256,1024]{2,1,0:T(8,128)(2,1)S(1)} %copy-done, f32[1024]{0:T(1024)S(1)} %bitcast.201, ...), kind=kOutput, calls=%fused_computation.52 | convolution fusion | flops 2218262528 | bytes 19425280 | tf_op jit(solution)/shard_map/dot_general | solution.py:139
  639.2 11.4 fusion.101
  651.9 5.9 convolution_convert_fusion.1
  658.0 7.2 convolution_convert_fusion
  669.7 41.7 %reduce-scatter.7.cloned.1.call-done = bf16[16,256,64]{1,2,0:T(8,128)(2,1)} async-done(((bf16[16,4096,64]{1,2,0:T(8,128)(2,1)}), bf16[16,256,64]{1,2,0:T(8,128)(2,1)}) %reduce-scatter.7.cloned.1.call-update) | async-done | bytes 524304 | tf_op jit(solution)/shard_map/reduce_scatter | solution.py:185
  714.8 105.3 %reduce-scatter.9.cloned.1.call-done = bf16[16,256,64]{1,2,0:T(8,128)(2,1)} async-done(((bf16[16,4096,64]{1,2,0:T(8,128)(2,1)}), bf16[16,256,64]{1,2,0:T(8,128)(2,1)}) %reduce-scatter.9.cloned.1.call-update) | async-done | bytes 524304 | tf_op jit(solution)/shard_map/reduce_scatter | solution.py:188
  820.1 5.8 convolution_convert_fusion.2
  825.9 96.0 %reduce-scatter.15.cloned.1.call-done = bf16[512,4096]{1,0:T(8,128)(2,1)} async-done(((bf16[1024,4096]{1,0:T(8,128)(2,1)}), bf16[512,4096]{1,0:T(8,128)(2,1)}) %reduce-scatter.15.cloned.1.call-update) | async-done | bytes 4194320 | tf_op jit(solution)/shard_map/reduce_scatter | solution.py:239
  922.0 101.5 %reduce-scatter.17.cloned.1.call-done = bf16[2048,1024]{1,0:T(8,128)(2,1)} async-done(((bf16[4096,1024]{1,0:T(8,128)(2,1)}), bf16[2048,1024]{1,0:T(8,128)(2,1)}) %reduce-scatter.17.cloned.1.call-update) | async-done | bytes 4194320 | tf_op jit(solution)/shard_map/reduce_scatter | solution.py:245
  1023.5 34.1 %reduce-scatter.13.cloned.1.call-done = bf16[512,1024]{1,0:T(8,128)(2,1)} async-done(((bf16[1024,1024]{1,0:T(8,128)(2,1)}), bf16[512,1024]{1,0:T(8,128)(2,1)}) %reduce-scatter.13.cloned.1.call-update) | async-done | bytes 1048592 | tf_op jit(solution)/shard_map/reduce_scatter | solution.py:233
  1057.6 79.9 %reduce-scatter.11.cloned.1.call-done = bf16[512,3072]{1,0:T(8,128)(2,1)} async-done(((bf16[1024,3072]{1,0:T(8,128)(2,1)}), bf16[512,3072]{1,0:T(8,128)(2,1)}) %reduce-scatter.11.cloned.1.call-update) | async-done | bytes 3145744 | tf_op jit(solution)/shard_map/reduce_scatter | solution.py:227
  1140.7 4.3 all-gather.3
  1145.0 4.5 all-gather.6
  1149.6 6.6 fusion.103
  1156.2 6.0 fusion.102
  1168.4 7.2 all-reduce.9
  1176.1 61.9 %all-reduce.7 = (bf16[512]{0:T(512)(128)(2,1)S(1)}, bf16[512]{0:T(512)(128)(2,1)S(1)}, bf16[512]{0:T(512)(128)(2,1)S(1)}, bf16[512]{0:T(512)(128)(2,1)S(1)}, bf1...) all-reduce(bf16[512]{0:T(512)(128)(2,1)S(1)} %dynamic-slice.1, ...), channel_id=1, replica_groups=mesh['ctx'=16,'fsdp'=2] {'ctx'}, use_global_device_ids=true, to_apply=%region_17.18 | all-reduce | flops 6144 | bytes 24576 | tf_op jit(solution)/shard_map/psum | solution.py:262
  1244.2 133.1 %all-reduce.12.cloned.1.call-done = (bf16[512,3072]{1,0:T(8,128)(2,1)}, bf16[512,1024]{1,0:T(8,128)(2,1)}, bf16[512,4096]{1,0:T(8,128)(2,1)}, bf16[2048,1024]{1,0:T(8,128)(2,1)}) async-done(((bf16[512,3072]{1,0:T(8,128)(2,1)}, bf16[512,1024]{1,0:T(8,128)(2,1)}, bf16[512,4096]{1,0:T(8,128)(2,1)}, bf16[2048,1024]{1,0:T(8,128)(2,1)}), (bf16[512,3072]{1,0:T(8,128)(2,1)}, bf16[512,1024]{1,0:T(8,128)(2,1)}, ...) | async-done | bytes 12582928 | tf_op jit(solution)/shard_map/psum | solution.py:266
  1377.3 6.8 convert_element_type.220
  1384.2 4.4 convert_element_type.223
  1388.6 3.5 convert_element_type.214
  (378 shorter events, 303.7 us)
Async XLA Ops:
  7.2 1.6 copy-start
  7.2 2.0 copy-start.19
  7.2 7.3 copy-start.20
  7.2 11.7 copy-start.18
  7.2 16.1 %copy-start.25 = (s32[32]{0:T(128)S(1)}, s32[32]{0:T(128)}, u32[]{:S(2)}) copy-start(s32[32]{0:T(128)} %param.33) | copy-start | bytes 388
  7.2 85.5 %all-gather.14.cloned.1.call-start = ((), (), s32[]{:S(2)}) async-start(), calls=%async_computation.6 | async-start | bytes 9437184 | tf_op jit(solution)/shard_map/all_gather | solution.py:81
  8.0 119.4 %all-gather.20.cloned.1.call-start = ((), (), s32[]{:S(2)}) async-start(), calls=%async_computation.9 | async-start | bytes 3145728 | tf_op jit(solution)/shard_map/all_gather | solution.py:83
  8.7 199.6 %all-gather.16.cloned.1.call-start = ((), (), s32[]{:S(2)}) async-start(), calls=%async_computation.7 | async-start | bytes 8912896 | tf_op jit(solution)/shard_map/all_gather | solution.py:118
  9.2 88.2 %copy-start.14 = (f32[256]{0:T(256)}, f32[256]{0:T(256)S(1)}, u32[]{:S(2)}) copy-start(f32[256]{0:T(256)S(1)} %fusion.64) | copy-start | bytes 3076
  97.4 1.7 copy-start.6
  105.3 178.7 %all-gather.18.cloned.1.call-start = ((), (), s32[]{:S(2)}) async-start(), calls=%async_computation.8 | async-start | bytes 8912896 | tf_op jit(solution)/shard_map/all_gather | solution.py:119
  107.5 20.0 %copy-start.1 = (bf16[1,256,1024]{2,1,0:T(8,128)(2,1)S(1)}, bf16[1,256,1024]{2,1,0:T(8,128)(2,1)}, u32[]{:S(2)}) copy-start(bf16[1,256,1024]{2,1,0:T(8,128)(2,1)} %param.20) | copy-start | bytes 1572868
  107.5 515.1 %all-gather.22.cloned.1.call-start = ((), (), s32[]{:S(2)}) async-start(), calls=%async_computation.10 | async-start | bytes 12582912 | tf_op jit(solution)/shard_map/all_gather | solution.py:85
  108.1 531.1 %all-gather.24.cloned.1.call-start = ((), (), s32[]{:S(2)}) async-start(), calls=%async_computation.11 | async-start | bytes 12582912 | tf_op jit(solution)/shard_map/all_gather | solution.py:87
  108.6 602.8 %reduce-scatter.7.cloned.1.call-start = ((), (), s32[]{:S(2)}) async-start(), calls=%async_computation.12 | async-start | bytes 8912896 | tf_op jit(solution)/shard_map/reduce_scatter | solution.py:185
  608.3 211.8 %reduce-scatter.9.cloned.1.call-start = ((), (), s32[]{:S(2)}) async-start(), calls=%async_computation.13 | async-start | bytes 8912896 | tf_op jit(solution)/shard_map/reduce_scatter | solution.py:188
  608.3 0.8 copy-start.21
  608.4 5.1 copy-start.22
  608.4 9.5 copy-start.17
  609.1 312.9 %reduce-scatter.15.cloned.1.call-start = ((), (), s32[]{:S(2)}) async-start(), calls=%async_computation.16 | async-start | bytes 12582912 | tf_op jit(solution)/shard_map/reduce_scatter | solution.py:239
  650.6 1.3 copy-start.10
  657.9 365.6 %reduce-scatter.17.cloned.1.call-start = ((), (), s32[]{:S(2)}) async-start(), calls=%async_computation.17 | async-start | bytes 12582912 | tf_op jit(solution)/shard_map/reduce_scatter | solution.py:245
  665.2 392.4 %reduce-scatter.13.cloned.1.call-start = ((), (), s32[]{:S(2)}) async-start(), calls=%async_computation.15 | async-start | bytes 3145728 | tf_op jit(solution)/shard_map/reduce_scatter | solution.py:233
  665.2 48.3 %copy-start.13 = (f32[256,16]{0,1:T(8,128)S(1)}, f32[256,16]{0,1:T(8,128)}, u32[]{:S(2)}) copy-start(f32[256,16]{0,1:T(8,128)} %get-tuple-element.309) | copy-start | bytes 49156
  667.4 470.1 %reduce-scatter.11.cloned.1.call-start = ((), (), s32[]{:S(2)}) async-start(), calls=%async_computation.14 | async-start | bytes 9437184 | tf_op jit(solution)/shard_map/reduce_scatter | solution.py:227
  714.8 111.1 %copy-start.8 = (bf16[256,16,64]{0,2,1:T(8,128)(2,1)}, bf16[256,16,64]{0,2,1:T(8,128)(2,1)S(1)}, u32[]{:S(2)}) copy-start(bf16[256,16,64]{0,2,1:T(8,128)(2,1)S(1)} %pad_maximum_fusion.4) | copy-start | bytes 1572868
  825.9 551.4 %all-reduce.12.cloned.1.call-start = ((), (), s32[]{:S(2)}) async-start(), calls=%async_computation.18 | async-start | bytes 25165824 | tf_op jit(solution)/shard_map/psum | solution.py:266
  1137.5 0.7 copy-start.26
  1137.5 3.2 copy-start.23
  1137.5 7.5 copy-start.24
  1149.6 6.6 copy-start.4
  1149.6 14.8 %slice-start = ((s8[6291456]{0:T(1024)(128)(4,1)}), s8[4194304]{0:T(1024)(128)(4,1)S(1)}, s32[]{:S(2)}) async-start(s8[6291456]{0:T(1024)(128)(4,1)} %bitcast.214), calls=%async_computation.19 | async-start | bytes 8388608
  1156.2 6.0 copy-start.7
  1156.2 8.1 slice-start.1
  1162.2 1.6 copy-start.9
  1162.2 1.6 copy-start.12
  1164.4 2.2 copy-start.15
  1166.6 1.0 copy-start.3
  1239.2 154.5 %copy-start.16 = (f32[512]{0:T(512)}, f32[512]{0:T(512)S(1)}, u32[]{:S(2)}) copy-start(f32[512]{0:T(512)S(1)} %convert_element_type.218) | copy-start | bytes 6148
  1377.3 6.8 copy-start.2
  1384.2 4.4 copy-start.5
  1388.6 3.5 copy-start.11
Sparse Core Ops, SparseCore 0:
  9.6 83.0 all-gather.13
  94.3 33.1 all-gather.19
  130.1 78.0 all-gather.15
  210.9 73.0 all-gather.17
  285.4 102.2 all-gather.21
  389.0 104.0 all-gather.23
  608.4 102.9 reduce-scatter.6
  715.5 104.5 reduce-scatter.8
  822.9 98.9 reduce-scatter.14
  924.2 99.2 reduce-scatter.16
  1025.7 31.8 reduce-scatter.12
  1060.4 77.0 reduce-scatter.10
  1142.0 235.2 all-reduce.11
where the time goes:
time: 1410 us; the launch traced here: 1400 us
  waiting for transfers between devices  824 us (58%)
  matrix products  329 us (23%)
  blocking collectives  105 us (7%)
  other arithmetic  58.5 us (4%)
  local copies, waits for them, and re-layouts  45.4 us (3%)
  loops' own time  21.9 us (2%)
  between operations  16.7 us (1%)
    dot_general x88, matrix products, contract(): lax.dot_general(left, right, (((left_dim,), (right_dim,)), ((), ())), pre...  206 us
    psum x1, waiting for transfers between devices, shards(): lax.psum(joint_part.astype(jnp.bfloat16), 'ctx').astype(jnp.float32)  133 us
    reduce_scatter x1, waiting for transfers between devices, shards(): lax.psum_scatter(value_grads.astype(jnp.bfloat16), 'ctx', scatter_dimensi...  105 us
    reduce_scatter x1, waiting for transfers between devices, shards(): lax.psum_scatter(shrink_grad.astype(jnp.bfloat16), 'fsdp', scatter_dimens...  102 us
    reduce_scatter x1, waiting for transfers between devices, shards(): lax.psum_scatter(expand_grad.astype(jnp.bfloat16), 'fsdp', scatter_dimens...  96 us
    reduce_scatter x1, waiting for transfers between devices, shards(): lax.psum_scatter(joint_grad.astype(jnp.bfloat16), 'fsdp', scatter_dimensi...  79.9 us
    all_gather x1, waiting for transfers between devices, shards(): lax.all_gather(key_rows, 'ctx', axis=0, tiled=True)  78.3 us
    all_gather x1, waiting for transfers between devices, shards(): lax.all_gather(joint_weight, 'fsdp', axis=0, tiled=True)  68.5 us
  transfers between devices with their start and end apart: 13, of which 11 were waited for; matrix products, arithmetic and copies ran while one was open for 29% of the time, Pallas kernels for 0%

commit v1 on v0

--- a/solution.py
+++ b/solution.py
@@ -1,6 +1,10 @@
+import functools
+
 import jax
 import jax.numpy as jnp
 from jax import lax
+from jax.experimental import pallas as pl
+from jax.experimental.pallas import tpu as pltpu
 from jax.sharding import PartitionSpec as P
 
 HEADS = 16
@@ -288,10 +292,629 @@
         column_total,
     )
 
+CYCLE = (0, 2, 4, 6, 7, 5, 3, 1)
+RIGHT = tuple(
+    (2 * CYCLE[i] + core, 2 * CYCLE[(i + 1) % 8] + core) for i in range(8) for core in range(2)
+)
+LEFT = tuple((b, a) for a, b in RIGHT)
+SWAP = tuple((i, i ^ 1) for i in range(16))
+OFFSETS = (0, -1, 1, -2, 2, -3, 3, 4)
+TILE = 512
+BLOCK = 128
+
+
+def right(values):
+    return lax.ppermute(values, "ctx", RIGHT)
+
+
+def left(values):
+    return lax.ppermute(values, "ctx", LEFT)
+
+
+def swap(values):
+    return lax.ppermute(values, "ctx", SWAP)
+
+
+def other(values):
+    return lax.ppermute(values, "fsdp", ((0, 1), (1, 0)))
+
+
+def after(values, *others):
+    return lax.optimization_barrier((values, *others))[0]
+
+
+def ring_gather(own):
+    half = own.shape[0] // 2
+    rights, lefts = [own], [own]
+    for _ in range(3):
+        rights.append(right(rights[-1]))
+        lefts.append(left(lefts[-1]))
+    far = jnp.concatenate([right(rights[3][:half]), left(lefts[3][half:])], 0)
+    pieces = [own]
+    for step in (1, 2, 3):
+        pieces += [rights[step], lefts[step]]
+    return pieces + [far]
+
+
+def ring_scatter(parts):
+    table = dict(zip(OFFSETS, parts))
+    half = parts[0].shape[0] // 2
+    add = lambda a, b: (a.astype(jnp.float32) + b.astype(jnp.float32)).astype(jnp.bfloat16)
+    ahead = right(table[4][:half])
+    behind = left(table[4][half:])
+    ahead = jnp.concatenate([add(ahead, table[3][:half]), table[3][half:]], 0)
+    behind = jnp.concatenate([table[-3][:half], add(behind, table[-3][half:])], 0)
+    for step in (2, 1):
+        ahead = add(right(ahead), table[step])
+        behind = add(left(behind), table[-step])
+    return right(ahead).astype(jnp.float32) + left(behind).astype(jnp.float32)
+
+
+def turn_back(values, lanes):
+    ahead = pltpu.roll(values, 128 - ROT // 2, 1)
+    behind = pltpu.roll(values, ROT // 2, 1)
+    return jnp.where(lanes % 64 < ROT // 2, -ahead, behind)
+
+
+def nt(left_side, right_side):
+    return lax.dot_general(
+        left_side, right_side, (((1,), (1,)), ((), ())), preferred_element_type=jnp.float32
+    )
+
+
+def nn(left_side, right_side):
+    return jnp.dot(left_side, right_side, preferred_element_type=jnp.float32)
+
+
+def forward_kernel(slots, joint, cosine, sine, mixed, q_out, k_out, v_out, o_out, lse_out):
+    rows = joint.shape[0]
+    tiles = rows // TILE
+    lanes = lax.broadcasted_iota(jnp.int32, (BLOCK, 128), 1)
+
+    def sort(p, _):
+        source = pl.ds(pl.multiple_of(slots[p] * BLOCK, BLOCK), BLOCK)
+        target = pl.ds(pl.multiple_of(p * BLOCK, BLOCK), BLOCK)
+        pair = joint[source, 0:128]
+        pair = pair * cosine[target, :] + turn_back(pair, lanes) * sine[target, :]
+        q_out[target, :] = pair[:, 0:64].astype(jnp.bfloat16)
+        k_out[target, :] = pair[:, 64:128].astype(jnp.bfloat16)
+        v_out[target, :] = joint[source, 128:192].astype(jnp.bfloat16)
+        return 0
+
+    lax.fori_loop(0, rows // BLOCK, sort, 0)
+    below = lax.broadcasted_iota(jnp.int32, (TILE, TILE), 0) <= lax.broadcasted_iota(
+        jnp.int32, (TILE, TILE), 1
+    )
+
+    def query_tile(i, _):
+        here = pl.ds(pl.multiple_of(i * TILE, TILE), TILE)
+        query = q_out[here, :] * jnp.bfloat16(0.125)
+
+        def step(j, carry, masked):
+            top, total, acc = carry
+            there = pl.ds(pl.multiple_of(j * TILE, TILE), TILE)
+            scores = nt(k_out[there, :], query)
+            if masked:
+                scores = jnp.where(below, scores, negative)
+            new_top = jnp.maximum(top, jnp.max(scores, 0, keepdims=True))
+            weights = jnp.exp(scores - new_top)
+            keep = jnp.exp(top - new_top)
+            total = total * keep + jnp.sum(weights, 0, keepdims=True)
+            term = lax.dot_general(
+                v_out[there, :],
+                weights.astype(jnp.bfloat16),
+                (((0,), (0,)), ((), ())),
+                preferred_element_type=jnp.float32,
+            )
+            return new_top, total, acc * keep + term
+
+        carry = (
+            jnp.full((1, TILE), negative, jnp.float32),
+            jnp.zeros((1, TILE), jnp.float32),
+            jnp.zeros((64, TILE), jnp.float32),
+        )
+        carry = lax.fori_loop(0, i, lambda j, c: step(j, c, False), carry)
+        top, total, acc = step(i, carry, True)
+        acc = acc / total
+        o_out[:, here] = acc
+        lse_out[:, here] = top + jnp.log(total)
+        out = acc.T.astype(jnp.bfloat16)
+        for part in range(TILE // BLOCK):
+            slot = slots[i * (TILE // BLOCK) + part]
+            mixed[pl.ds(pl.multiple_of(slot * BLOCK, BLOCK), BLOCK), :] = out[
+                part * BLOCK : (part + 1) * BLOCK
+            ]
+        return 0
+
+    lax.fori_loop(0, tiles, query_tile, 0)
+
+
+def backward_kernel(
+    slots, q_in, k_in, v_in, o_in, lse_in, mixed_grad, cosine, sine, delta_out, grad_sorted, inner, dq, dk, dv
+):
+    rows = q_in.shape[0]
+    tiles = rows // TILE
+    lanes = lax.broadcasted_iota(jnp.int32, (BLOCK, 128), 1)
+
+    def sort(p, _):
+        source = pl.ds(pl.multiple_of(slots[p] * BLOCK, BLOCK), BLOCK)
+        target = pl.ds(pl.multiple_of(p * BLOCK, BLOCK), BLOCK)
+        piece = mixed_grad[source, :]
+        grad_sorted[target, :] = piece
+        flat = piece.astype(jnp.float32).T
+        inner[:, target] = jnp.sum(flat * o_in[:, target], 0, keepdims=True)
+        return 0
+
+    lax.fori_loop(0, rows // BLOCK, sort, 0)
+    dq[...] = jnp.zeros_like(dq)
+    below = lax.broadcasted_iota(jnp.int32, (TILE, TILE), 0) <= lax.broadcasted_iota(
+        jnp.int32, (TILE, TILE), 1
+    )
+
+    def key_tile(j, _):
+        there = pl.ds(pl.multiple_of(j * TILE, TILE), TILE)
+        key = k_in[there, :]
+        value = v_in[there, :]
+
+        def step(i, carry, masked):
+            key_grad, value_grad = carry
+            here = pl.ds(pl.multiple_of(i * TILE, TILE), TILE)
+            query = q_in[here, :] * jnp.bfloat16(0.125)
+            grad = grad_sorted[here, :]
+            scores = nt(key, query)
+            probs = jnp.exp(scores - lse_in[:, here])
+            if masked:
+                probs = jnp.where(below, probs, 0.0)
+            prob_grad = nt(value, grad)
+            score_grad = (probs * (prob_grad - inner[:, here])).astype(jnp.bfloat16)
+            value_grad = value_grad + nn(probs.astype(jnp.bfloat16), grad)
+            key_grad = key_grad + nn(score_grad, query)
+            dq[:, here] += lax.dot_general(
+                key, score_grad, (((0,), (0,)), ((), ())), preferred_element_type=jnp.float32
+            )
+            return key_grad, value_grad
+
+        zero = jnp.zeros((TILE, 64), jnp.float32)
+        carry = step(j, (zero, zero), True)
+        key_grad, value_grad = lax.fori_loop(
+            j + 1, tiles, lambda i, c: step(i, c, False), carry
+        )
+        dk[there, :] = key_grad
+        dv[there, :] = value_grad
+        return 0
+
+    lax.fori_loop(0, tiles, key_tile, 0)
+
+    def finish(p, _):
+        target = pl.ds(pl.multiple_of(slots[p] * BLOCK, BLOCK), BLOCK)
+        source = pl.ds(pl.multiple_of(p * BLOCK, BLOCK), BLOCK)
+        pair = jnp.concatenate([dq[:, source].T * 0.125, dk[source, :]], 1)
+        pair = pair * cosine[source, :] - turn_back(pair, lanes) * sine[source, :]
+        delta_out[target, 0:128] = pair.astype(jnp.bfloat16)
+        value = dv[source, :]
+        delta_out[target, 128:256] = jnp.concatenate(
+            [value, jnp.zeros_like(value)], 1
+        ).astype(jnp.bfloat16)
+        return 0
+
+    lax.fori_loop(0, rows // BLOCK, finish, 0)
+
+
+def whole(count):
+    return [pl.BlockSpec(memory_space=pltpu.VMEM)] * count
+
+
+def attention_forward(slots, joint, cosine, sine):
+    rows = joint.shape[0]
+    head = jax.ShapeDtypeStruct((rows, 64), jnp.bfloat16)
+    return pl.pallas_call(
+        forward_kernel,
+        in_specs=[pl.BlockSpec(memory_space=pltpu.SMEM)] + whole(3),
+        out_specs=whole(6),
+        out_shape=[
+            head,
+            head,
+            head,
+            head,
+            jax.ShapeDtypeStruct((64, rows), jnp.float32),
+            jax.ShapeDtypeStruct((1, rows), jnp.float32),
+        ],
+        compiler_params=pltpu.CompilerParams(vmem_limit_bytes=48 * 1024 * 1024),
+        cost_estimate=pl.CostEstimate(
+            flops=rows * rows * 512, bytes_accessed=rows * 4096, transcendentals=rows * rows // 2
+        ),
+        name="attention_forward",
+    )(slots, joint, cosine, sine)
+
+
+def attention_backward(slots, query, key, value, out, lse, mixed_grad, cosine, sine):
+    rows = query.shape[0]
+    return pl.pallas_call(
+        backward_kernel,
+        in_specs=[pl.BlockSpec(memory_space=pltpu.SMEM)] + whole(8),
+        out_specs=pl.BlockSpec(memory_space=pltpu.VMEM),
+        out_shape=jax.ShapeDtypeStruct((rows, 256), jnp.bfloat16),
+        scratch_shapes=[
+            pltpu.VMEM((rows, 64), jnp.bfloat16),
+            pltpu.VMEM((1, rows), jnp.float32),
+            pltpu.VMEM((64, rows), jnp.float32),
+            pltpu.VMEM((rows, 64), jnp.float32),
+            pltpu.VMEM((rows, 64), jnp.float32),
+        ],
+        compiler_params=pltpu.CompilerParams(vmem_limit_bytes=48 * 1024 * 1024),
+        cost_estimate=pl.CostEstimate(
+            flops=rows * rows * 1280, bytes_accessed=rows * 4096, transcendentals=rows * rows // 2
+        ),
+        name="attention_backward",
+    )(slots, query, key, value, out, lse, mixed_grad, cosine, sine)
+
+
+def assemble_kernel(count, owners, *refs):
+    blobs = refs[:count]
+    shrink, dense, expand = refs[count + 3 : count + 6]
+    wide, tall, sems = refs[count + 6 :]
+    group = owners[count]
+    hidden = expand.shape[1] // 2
+
+    def dense_copy(n, owner):
+        return pltpu.make_async_copy(
+            wide.at[n, pl.ds(128, 64)],
+            dense.at[pl.ds(pl.multiple_of(lax.rem(owner, 8) * 64, 64), 64)],
+            sems.at[n, 3],
+        )
+
+    copies = []
+    for n in range(count):
+        owner = owners[n]
+        blob = blobs[n]
+        wide[n] = blob[0:192, :].astype(jnp.float32)
+        for quarter in range(4):
+            tall[n, quarter * 128 : (quarter + 1) * 128, :] = blob[
+                192:320, quarter * 256 : (quarter + 1) * 256
+            ].astype(jnp.float32)
+        start = pl.multiple_of(owner * 128, 128)
+        copies.append(
+            pltpu.make_async_copy(
+                wide.at[n, pl.ds(0, 128)], shrink.at[pl.ds(start, 128)], sems.at[n, 0]
+            )
+        )
+        copies.append(
+            pltpu.make_async_copy(
+                tall.at[n, :, pl.ds(0, 128)], expand.at[:, pl.ds(start, 128)], sems.at[n, 1]
+            )
+        )
+        copies.append(
+            pltpu.make_async_copy(
+                tall.at[n, :, pl.ds(128, 128)],
+                expand.at[:, pl.ds(pl.multiple_of(hidden + start, 128), 128)],
+                sems.at[n, 2],
+            )
+        )
+        for copy in copies[-3:]:
+            copy.start()
+
+        @pl.when(owner // 8 == group)
+        def _(n=n, owner=owner):
+            dense_copy(n, owner).start()
+
+    for copy in copies:
+        copy.wait()
+    for n in range(count):
+        owner = owners[n]
+
+        @pl.when(owner // 8 == group)
+        def _(n=n, owner=owner):
+            dense_copy(n, owner).wait()
+
+
+def assemble(owners, blobs, outs):
+    count = len(blobs)
+    anywhere = [pl.BlockSpec(memory_space=pl.ANY)] * 3
+    return pl.pallas_call(
+        functools.partial(assemble_kernel, count),
+        in_specs=[pl.BlockSpec(memory_space=pltpu.SMEM)] + whole(count) + anywhere,
+        out_specs=anywhere,
+        out_shape=[jax.ShapeDtypeStruct(o.shape, o.dtype) for o in outs],
+        scratch_shapes=[
+            pltpu.VMEM((count, 192, 1024), jnp.float32),
+            pltpu.VMEM((count, 512, 256), jnp.float32),
+            pltpu.SemaphoreType.DMA((count, 4)),
+        ],
+        input_output_aliases={1 + count + i: i for i in range(3)},
+        compiler_params=pltpu.CompilerParams(vmem_limit_bytes=48 * 1024 * 1024),
+        cost_estimate=pl.CostEstimate(
+            flops=0, bytes_accessed=count * 320 * 1024 * 6, transcendentals=0
+        ),
+        name="assemble_blobs",
+    )(owners, *blobs, *outs)
+
+
+def assemble_joint_kernel(count, owners, *refs):
+    blobs = refs[:count]
+    joint = refs[count + 1]
+    buffer, sems = refs[count + 2 :]
+    width = joint.shape[1] // 3
+    copies = []
+    for n in range(count):
+        owner = owners[n]
+        buffer[n] = blobs[n][...].astype(jnp.float32)
+        for part in range(3):
+            start = pl.multiple_of(part * width + (owner // 2) * 128, 128)
+            top = pl.multiple_of(lax.rem(owner, 2) * 256, 256)
+            copies.append(
+                pltpu.make_async_copy(
+                    buffer.at[n, :, pl.ds(part * 128, 128)],
+                    joint.at[pl.ds(top, 256), pl.ds(start, 128)],
+                    sems.at[n, part],
+                )
+            )
+            copies[-1].start()
+    for copy in copies:
+        copy.wait()
+
+
+def assemble_joint(owners, blobs, out):
+    count = len(blobs)
+    return pl.pallas_call(
+        functools.partial(assemble_joint_kernel, count),
+        in_specs=[pl.BlockSpec(memory_space=pltpu.SMEM)]
+        + whole(count)
+        + [pl.BlockSpec(memory_space=pl.ANY)],
+        out_specs=pl.BlockSpec(memory_space=pl.ANY),
+        out_shape=jax.ShapeDtypeStruct(out.shape, out.dtype),
+        scratch_shapes=[
+            pltpu.VMEM((count, 256, 384), jnp.float32),
+            pltpu.SemaphoreType.DMA((count, 3)),
+        ],
+        input_output_aliases={1 + count: 0},
+        compiler_params=pltpu.CompilerParams(vmem_limit_bytes=48 * 1024 * 1024),
+        cost_estimate=pl.CostEstimate(
+            flops=0, bytes_accessed=count * 256 * 384 * 6, transcendentals=0
+        ),
+        name="assemble_joint",
+    )(owners, *blobs, out)
+
+
+def split_heads(
+    tokens,
+    cotangent,
+    first_gain,
+    first_shift,
+    second_gain,
+    second_shift,
+    joint_weight,
+    joint_bias,
+    dense_weight,
+    dense_bias,
+    expand_weight,
+    expand_bias,
+    shrink_weight,
+    shrink_bias,
+    block_order,
+):
+    f32, bf16 = jnp.float32, jnp.bfloat16
+    me = lax.axis_index("ctx")
+    group = lax.axis_index("fsdp")
+    rows, width = tokens.shape[1:]
+    total_rows = rows * 16
+    hidden = expand_weight.shape[1] // 2
+    own_tokens, own_upstream = tokens[0], cotangent[0]
+
+    def cut(values, start, size, axis):
+        return lax.dynamic_slice_in_dim(values, start, size, axis)
+
+    def both(values, axis):
+        received = other(values)
+        lower = jnp.where(group == 0, values, received)
+        upper = jnp.where(group == 0, received, values)
+        return jnp.concatenate([lower, upper], axis)
+
+    cycle = jnp.array(CYCLE, jnp.int32)
+    place = jnp.array([CYCLE.index(i) for i in range(8)], jnp.int32)[me // 2]
+    chips = cycle[(place + jnp.array(OFFSETS, jnp.int32)) % 8]
+    owners = jnp.concatenate([2 * chips + me % 2, 2 * chips + 1 - me % 2])
+    blocks = block_order.reshape(16, 2)[owners].reshape(32)
+    slots = jnp.zeros((32,), jnp.int32).at[blocks].set(jnp.arange(32, dtype=jnp.int32))
+
+    vectors = both(
+        jnp.concatenate(
+            [
+                v.reshape(-1, 512)
+                for v in (
+                    first_gain,
+                    first_shift,
+                    second_gain,
+                    second_shift,
+                    dense_bias,
+                    shrink_bias,
+                    joint_bias,
+                    expand_bias,
+                )
+            ],
+            0,
+        )[None],
+        0,
+    )
+    gain_one, shift_one, gain_two, shift_two, dense_shift, shrink_shift = (
+        vectors[:, i, :].reshape(-1).astype(f32) for i in range(6)
+    )
+    joint_shift = vectors[:, 6:9, :].reshape(3, 16, 64)
+    expand_shift = vectors[:, 9:13, :].reshape(2, 16, 128)
+    joint_part = cut(joint_weight.reshape(-1, 3, 16, 64), me, 1, 2).reshape(-1, 192)
+    joint_c = both(jnp.pad(joint_part, ((0, 0), (0, 64))), 0)
+    joint_b = jnp.pad(cut(joint_shift, me, 1, 1).reshape(192), (0, 64)).astype(f32)
+    expand_part = jnp.concatenate(
+        [cut(expand_weight, me * 128, 128, 1), cut(expand_weight, hidden + me * 128, 128, 1)], 1
+    )
+    expand_c = both(expand_part, 0)
+    expand_b = cut(expand_shift, me, 1, 1).reshape(256).astype(f32)
+    shrink_c = both(cut(shrink_weight, me * 128, 128, 0), 0)
+    dense_part = cut(dense_weight, (me % 8) * 64, 64, 0)
+    dense_c = jnp.where(group == me // 8, dense_part, other(dense_part))
+
+    token_own = ring_gather(own_tokens)
+    token_all = token_own + [swap(v) for v in token_own]
+    inputs = jnp.concatenate(token_all, 0)
+    upstream_own = ring_gather(after(own_upstream, token_own[-2], token_own[-3]))
+    upstream = jnp.concatenate(upstream_own + [swap(v) for v in upstream_own], 0)
+
+    wide = inputs.astype(f32)
+    center = wide - jnp.mean(wide, -1, keepdims=True)
+    spread = jnp.mean(center * center, -1, keepdims=True)
+    unit = center * lax.rsqrt(spread + epsilon)
+    normed_one = (unit * gain_one + shift_one).astype(bf16)
+    normed_two = (unit * gain_two + shift_two).astype(bf16)
+    joint = nn(normed_one, joint_c) + joint_b
+    expanded = nn(normed_two, expand_c) + expand_b
+    activated = jax.nn.gelu(expanded, approximate=False).astype(bf16)
+
+    inverse = jnp.power(10000.0, -2.0 * jnp.arange(ROT // 2, dtype=f32) / ROT)
+    angles = jnp.arange(total_rows, dtype=f32)[:, None] * inverse[None, :]
+    rest = jnp.zeros((total_rows, 64 - ROT), f32)
+    cosine = jnp.concatenate([jnp.cos(angles), jnp.cos(angles), rest + 1.0] * 2, 1)
+    sine = jnp.concatenate([jnp.sin(angles), jnp.sin(angles), rest] * 2, 1)
+
+    mixed, query, key, value, out, lse = attention_forward(slots, joint, cosine, sine)
+
+    branch = jnp.concatenate([activated, mixed], 1)
+    back = jnp.concatenate([shrink_c, dense_c], 0)
+    out_parts = core_sums(branch, back)
+    out_sum = out_parts[0].astype(f32) + ring_scatter(out_parts)
+    output = own_tokens.astype(f32) + out_sum + dense_shift + shrink_shift
+
+    column_sum = jnp.sum(upstream.astype(f32), 0)
+    back_grad = contract(branch, upstream, 0, 0)
+    act_grad = nt(upstream, shrink_c)
+    mixed_grad = nt(upstream, dense_c).astype(bf16)
+    _, gelu_pull = jax.vjp(lambda v: jax.nn.gelu(v, approximate=False), expanded)
+    expand_delta = gelu_pull(act_grad)[0].astype(bf16)
+    expand_grad = contract(normed_two, expand_delta, 0, 0)
+    expand_sum = jnp.sum(expand_delta.astype(f32), 0)
+
+    def half_of(values, which, axis):
+        size = values.shape[axis] // 2
+        return cut(values, which * size, size, axis)
+
+    def sum_halves(values, axis):
+        sent = half_of(values, 1 - group, axis).astype(bf16)
+        return half_of(values, group, axis) + other(sent).astype(f32)
+
+    shrink_half = sum_halves(back_grad[:256], 0).astype(bf16)
+    dense_half = (back_grad[256:] + other(back_grad[256:].astype(bf16)).astype(f32)).astype(bf16)
+    expand_half = sum_halves(expand_grad, 0).astype(bf16)
+    blob = jnp.concatenate(
+        [
+            shrink_half,
+            dense_half,
+            jnp.concatenate([expand_half[i * 128 : (i + 1) * 128] for i in range(4)], 1),
+        ],
+        0,
+    )
+    blob_own = ring_gather(blob)
+    blob_all = blob_own + [swap(v) for v in blob_own]
+    outs = tuple(
+        jnp.zeros(shape, f32) for shape in ((hidden, width), (width // 2, width), (width // 2, 2 * hidden))
+    )
+    for start in (0, 4, 8, 12):
+        some = owners[start : start + 4]
+        outs = assemble(jnp.concatenate([some, group[None]]), blob_all[start : start + 4], outs)
+    shrink_total, dense_total, expand_total = outs
+
+    joint_delta = attention_backward(
+        slots, query, key, value, out, lse, mixed_grad, cosine, sine
+    )
+    joint_grad = contract(normed_one, joint_delta, 0, 0)
+    joint_sum = jnp.sum(joint_delta.astype(f32), 0)
+
+    delta = jnp.concatenate([joint_delta, expand_delta], 1)
+    scaled = jnp.concatenate(
+        [
+            (joint_c.astype(f32) * gain_one[:, None]).astype(bf16),
+            (expand_c.astype(f32) * gain_two[:, None]).astype(bf16),
+        ],
+        1,
+    ).T
+    in_parts = core_sums(delta, scaled)
+    in_sum = in_parts[0].astype(f32) + ring_scatter(in_parts)
+    mine = own_tokens.astype(f32)
+    mine = mine - jnp.mean(mine, -1, keepdims=True)
+    scale = lax.rsqrt(jnp.mean(mine * mine, -1, keepdims=True) + epsilon)
+    mine = mine * scale
+    term = scale * (
+        in_sum
+        - jnp.mean(in_sum, -1, keepdims=True)
+        - mine * jnp.mean(in_sum * mine, -1, keepdims=True)
+    )
+    tokens_grad = (own_upstream.astype(f32) + term).astype(bf16)
+
+    joint_half = sum_halves(joint_grad, 0)[:, :192].astype(bf16)
+    core = me % 2
+    kept = half_of(joint_half, core, 0)
+    received = swap(half_of(joint_half, 1 - core, 0))
+    low = jnp.where(core == 0, kept, received).reshape(-1, 3, 1, 64)
+    high = jnp.where(core == 0, received, kept).reshape(-1, 3, 1, 64)
+    joint_blob = jnp.concatenate([low, high], 2).reshape(-1, 384)
+    joint_own = ring_gather(joint_blob)
+    joint_all = joint_own + [swap(v) for v in joint_own]
+    joint_total = jnp.zeros((width // 2, 3 * width), f32)
+    joint_total = assemble_joint(owners, joint_all, joint_total)
+
+    def norm_grads(weight, grad, total, gain, shift):
+        weight = weight.astype(f32)
+        shift_grad = jnp.sum(weight * total[None, :], 1)
+        return (jnp.sum(weight * grad, 1) - shift * shift_grad) / gain, shift_grad
+
+    gain_one_grad, shift_one_grad = norm_grads(joint_c, joint_grad, joint_sum, gain_one, shift_one)
+    gain_two_grad, shift_two_grad = norm_grads(expand_c, expand_grad, expand_sum, gain_two, shift_two)
+    mark = (jnp.arange(16) == me).astype(f32)[None, :, None]
+    expand_bias = (mark * expand_sum.reshape(2, 1, 128)).reshape(-1)
+    joint_bias_all = (mark * joint_sum[:192].reshape(3, 1, 64)).reshape(-1)
+    early = lax.psum(
+        jnp.concatenate([expand_bias, gain_two_grad, shift_two_grad, column_sum / 16]),
+        ("ctx", "fsdp"),
+    )
+    late = lax.psum(
+        jnp.concatenate([joint_bias_all, gain_one_grad, shift_one_grad]), ("ctx", "fsdp")
+    )
+
+    def shard(values, start, size):
+        return cut(values, start + group * (size // 2), size // 2, 0)
+
+    full = 2 * hidden
+    column_total = shard(early, full + 2 * width, width)
+    return (
+        output.astype(bf16)[None],
+        tokens_grad[None],
+        shard(late, 3 * width, width),
+        shard(late, 4 * width, width),
+        shard(early, full, width),
+        shard(early, full + width, width),
+        joint_total,
+        shard(late, 0, 3 * width),
+        dense_total,
+        column_total,
+        expand_total,
+        shard(early, 0, full),
+        shrink_total,
+        column_total,
+    )
+
+
+def core_sums(values, weight):
+    rows = values.shape[0] // 16
+    parts = []
+    for first, last in ((7, 8), (5, 7), (3, 5), (1, 3), (0, 1)):
+        theirs = nn(values[(8 + first) * rows : (8 + last) * rows], weight).astype(jnp.bfloat16)
+        mine = nn(values[first * rows : last * rows], weight)
+        both = (mine + swap(theirs).astype(jnp.float32)).astype(jnp.bfloat16)
+        parts = [both[i * rows : (i + 1) * rows] for i in range(last - first)] + parts
+    return parts
+
 
 def solution(mesh):
+    fits = mesh.shape["ctx"] == HEADS and mesh.shape["fsdp"] == 2
     return jax.shard_map(
-        shards,
+        split_heads if fits else shards,
         mesh=mesh,
         in_specs=(
             P("fsdp", "ctx", None),

time: 1410 us -> 589 us (0.42)
  waiting for transfers between devices: 824 us -> 128 us
  matrix products: 329 us -> 72.4 us
  Pallas kernels: 0 us -> 94.8 us
  local copies, waits for them, and re-layouts: 45.4 us -> 112 us
  starting transfers between devices: 0.7 us -> 65.6 us
  blocking collectives: 105 us -> 50.8 us
  loops' own time: 21.9 us -> 0 us
  between operations: 16.7 us -> 2.57 us
    reduce_scatter x6 -> x0, waiting for transfers between devices: 459 us -> none  [the longest x1 105 us: shards(): lax.psum_scatter(value_grads.astype(jnp.bfloat16), 'ctx', scatter_dimensi...]
    all_gather x6 -> x0, waiting for transfers between devices: 229 us -> none  [the longest x1 78.3 us: shards(): lax.all_gather(key_rows, 'ctx', axis=0, tiled=True)]
    dot_general x88 -> x3, matrix products: 206 us -> 14.8 us  [contract(): lax.dot_general(left, right, (((left_dim,), (right_dim,)), ((), ())), pre...]
    psum x1 -> x0, waiting for transfers between devices: 133 us -> none  [shards(): lax.psum(joint_part.astype(jnp.bfloat16), 'ctx').astype(jnp.float32)]
    ppermute x0 -> x100, waiting for transfers between devices: none -> 128 us  [the longest x24 77.7 us: right(): return lax.ppermute(values, 'ctx', RIGHT)]
    pallas_call x0 -> x7, Pallas kernels: none -> 94.8 us  [the longest x1 44.6 us: attention_backward(): pl.pallas_call(backward_kernel, in_specs=[pl.BlockSpec(memory_space=pltpu...]
    ppermute x0 -> x100, starting transfers between devices: none -> 65.6 us  [the longest x24 33.2 us: right(): return lax.ppermute(values, 'ctx', RIGHT)]
    dot_general x36 -> x24, matrix products: 123 us -> 57.6 us  [the longest x22 48.2 us: nn(): return jnp.dot(left_side, right_side, preferred_element_type=jnp.float32)]
  transfers between devices with their start and end apart: 13 -> 100, of which waited for: 11 -> 35; matrix products, arithmetic and copies ran while one was open for 29% -> 38% of each run, Pallas kernels for 0% -> 16%
where the time goes in v1:
time: 589 us; the launch traced here: 580 us
  waiting for transfers between devices  128 us (22%)
  local copies, waits for them, and re-layouts  112 us (19%)
  Pallas kernels  94.8 us (16%)
  matrix products  72.4 us (12%)
  starting transfers between devices  65.6 us (11%)
  other arithmetic  53.9 us (9%)
  blocking collectives  50.8 us (9%)
    ppermute x24, waiting for transfers between devices, right(): return lax.ppermute(values, 'ctx', RIGHT)  77.7 us
    psum x1, blocking collectives, split_heads(): lax.psum(jnp.concatenate([joint_bias_all, gain_one_grad, shift_one_grad])...  50.8 us
    dot_general x22, matrix products, nn(): return jnp.dot(left_side, right_side, preferred_element_type=jnp.float32)  48.2 us
    unnamed x208, local copies, waits for them, and re-layouts  45.4 us
    pallas_call x1, Pallas kernels, attention_backward(): pl.pallas_call(backward_kernel, in_specs=[pl.BlockSpec(memory_space=pltpu...  44.6 us
    ppermute x24, waiting for transfers between devices, left(): return lax.ppermute(values, 'ctx', LEFT)  33.8 us
    pallas_call x1, Pallas kernels, attention_forward(): pl.pallas_call(forward_kernel, in_specs=[pl.BlockSpec(memory_space=pltpu....  33.3 us
    ppermute x24, starting transfers between devices, right(): return lax.ppermute(values, 'ctx', RIGHT)  33.2 us
  transfers between devices with their start and end apart: 100, of which 35 were waited for; matrix products, arithmetic and copies ran while one was open for 38% of the time, Pallas kernels for 16%

profile of v1, /device:TPU:0, one launch (start us, length us, event | category | flops | bytes accessed | tf_op | source)
XLA Modules:
  0.0 579.6 jit_solution(14192041144029593606)
XLA Ops:
  0.7 3.1 collective-permute-start
  11.4 4.7 copy.70
  22.3 8.6 %fusion.19 = (f32[4096,8]{1,0:T(8,128)S(1)}, f32[4096,8]{1,0:T(8,128)}) fusion(f32[8]{0:T(128)S(1)} %multiply_power_fusion), kind=kLoop, calls=%fused_computation.48 | loop fusion | flops 32768 | bytes 262176 | tf_op jit(solution)/shard_map/sin | solution.py:775
  37.4 10.8 %concatenate.134.cosine = f32[4096,128]{1,0:T(8,128)} concatenate(f32[4096,8]{1,0:T(8,128)} %get-tuple-element.119, f32[4096,8]{1,0:T(8,128)} %get-tuple-element.119, f32[4096,48]{1,0:T(8,128)} %add.366, f32[4096,8]{1,0:T(8,128)} %get-tuple-element.119, f32[4096,8]{1,0:T(8,128)} %get-tuple-element.119, f32[4096,48]{1,0:T(8,128)} %add.366), dimensions={1} | concatenate | bytes 4194304 | tf_op jit(solution)/shard_map/concatenate | solution.py:774
  49.7 7.8 %concatenate.135.sine = f32[4096,128]{1,0:T(8,128)} concatenate(f32[4096,8]{1,0:T(8,128)S(1)} %get-tuple-element.118, f32[4096,8]{1,0:T(8,128)S(1)} %get-tuple-element.118, f32[4096,48]{1,0:T(8,128)} %broadcast_in_dim.22, f32[4096,8]{1,0:T(8,128)S(1)} %get-tuple-element.118, f32[4096,8]{1,0:T(8,128)S(1)} %get-tuple-element.118, f32[4096,48]{1,0:T(8,128)} %broadcast_in_dim.22), dimensions={1} | concatenate | bytes 4194304 | tf_op jit(solution)/shard_map/concatenate | solution.py:775
  60.3 2.7 collective-permute-done.20
  73.2 4.4 collective-permute-done.2
  86.7 2.6 collective-permute-done.4
  106.7 6.9 %collective-permute-done.34 = bf16[256,1024]{1,0:T(8,128)(2,1)} collective-permute-done((bf16[256,1024]{1,0:T(8,128)(2,1)}, bf16[256,1024]{1,0:T(8,128)(2,1)}, u32[]{:S(2)}, u32[]{:S(2)}) %collective-permute-start.34) | collective-permute-done | bytes 524320 | tf_op jit(solution)/shard_map/ppermute | solution.py:307
  122.4 4.7 convert_reduce_fusion
  128.2 2.9 fusion.8
  131.1 6.2 %fusion.5 = (bf16[4096,1024]{1,0:T(8,128)(2,1)}, bf16[4096,1024]{1,0:T(8,128)(2,1)S(1)}) fusion(bf16[4096,1024]{1,0:T(8,128)(2,1)S(1)} %copy-done.34, f32[1024]{0:T(1024)S(1)} %bitcast.71, f32[1024]{0:T(1024)S(1)} %bitcast.68, f32[4096]{0:T(1024)S(1)} %add_rsqrt_fusion, f32[4096]{0:T(1024)S(1)} %broadcast_multiply_fusion.2, f32[1024]{0:T(1024)S(1)} %bitcast.76, ...), kind=kLoop, calls=%fused_computation.10 | loop fusion | flops 37748736 | bytes 25214976 | tf_op jit(solution)/shard_map/convert_element_type | solution.py:766
  137.4 3.4 copy-done.51
  140.7 4.5 convolution_add_fusion.joint
  145.2 33.3 %attention_forward.1 = (bf16[4096,64]{1,0:T(8,128)(2,1)S(1)}, bf16[4096,64]{1,0:T(8,128)(2,1)S(1)}, bf16[4096,64]{1,0:T(8,128)(2,1)S(1)}, bf16[4096,64]{1,0:T(8,...) custom-call(s32[32]{0:T(128)S(1)} %scatter_custom_fusion.slots, f32[4096,256]{1,0:T(8,128)} %convolution_add_fusion.joint, ...), custom_call_target="tpu_custom_call" | custom-call | flops 8589934592 | bytes 16777216 | tf_op jit(solution)/shard_map/attention_forward/pallas_call | solution.py:510
  178.6 15.6 %multiply_convert_fusion = (bf16[4096,256]{1,0:T(8,128)(2,1)S(1)}, f32[4096,256]{1,0:T(8,128)}, f32[4096,256]{1,0:T(8,128)}) fusion(f32[256]{0:T(256)S(1)} %bitcast.84, bf16[4096,1024]{1,0:T(8,128)(2,1)} %get-tuple-element.63, bf16[512,256]{0,1:T(8,128)(2,1)S(1)} %copy-done.66, bf16[512,256]{0,1:T(8,128)(2,1)S(1)} %copy-done.64), kind=kOutput, calls=%fused_computation.23 | convolution fusion | flops 2217738240 | bytes 19399680 | tf_op jit(solution)/shard_map/dot_general | solution.py:366
  203.9 8.9 %collective-permute-done.38 = bf16[256,1024]{1,0:T(8,128)(2,1)S(1)} collective-permute-done((bf16[256,1024]{1,0:T(8,128)(2,1)}, bf16[256,1024]{1,0:T(8,128)(2,1)S(1)}, u32[]{:S(2)}, u32[]{:S(2)}) %collective-permute-start.38) | collective-permute-done | bytes 524320 | tf_op jit(solution)/shard_map/ppermute | solution.py:307
  217.4 4.2 collective-permute-done.23
  240.0 3.4 copy-done.41
  243.3 3.5 convolution_convert_fusion
  252.0 44.6 %attention_backward.1 = bf16[4096,256]{1,0:T(8,128)(2,1)} custom-call(s32[32]{0:T(128)S(1)} %scatter_custom_fusion.slots, bf16[4096,64]{1,0:T(8,128)(2,1)S(1)} %get-tuple-element.34.q_in, bf16[4096,64]{1,0:T(8,128)(2,1)S(1)} %copy-done.19, bf16[4096,64]{1,0:T(8,128)(2,1)S(1)} %copy-done.21, f32[64,4096]{1,0:T(8,128)S(1)} %copy-done.23, ...), custom_call_target="tpu_custom_call" | custom-call | flops 21474836480 | bytes 16777216 | tf_op jit(solution)/shard_map/attention_backward/pallas_call | solution.py:532
  299.0 7.5 %fusion.40 = (f32[1024]{0:T(1024)S(1)}, f32[1024]{0:T(1024)S(1)}, bf16[1024,256]{0,1:T(8,128)(2,1)S(1)}, f32[1024,256]{0,1:T(8,128)}) fusion(bf16[512,256]{0,1:T(8,128)(2,1)S(1)} %copy-done.63, bf16[512,256]{0,1:T(8,128)(2,1)S(1)} %copy-done.61, f32[256]{0:T(256)S(1)} %convert_reduce_fusion.3, f32[1024]{0:T(1024)S(1)} %bitcast.74, ...), kind=kOutput, calls=%fused_computation.90 | convolution fusion | flops 2150103040 | bytes 12596224 | tf_op jit(solution)/shard_map/dot_general | solution.py:39
  306.5 5.9 %convert_reduce_fusion.2 = (f32[256]{0:T(256)S(1)}, bf16[4096,256]{1,0:T(8,128)(2,1)S(1)}) fusion(f32[4096,256]{1,0:T(8,128)S(1)} %copy-done.79, f32[4096,256]{1,0:T(8,128)} %get-tuple-element.122, bf16[4096,1024]{1,0:T(8,128)(2,1)S(1)} %bitcast.54, bf16[128,1024]{1,0:T(8,128)(2,1)S(1)} %copy-done.45, bf16[128,1024]{1,0:T(8,128)(2,1)S(1)} %get-tuple-element.89), kind=kOutput, calls=%fused_computation.20 | convolution fusion | flops 2165309184 | bytes 19399680 | tf_op jit(solution)/shard_map/dot_general | solution.py:360
  312.5 3.4 fusion.43
  320.6 3.9 fusion.15
  347.6 5.0 collective-permute-done.83
  352.7 3.2 collective-permute-done.81
  361.9 3.0 collective-permute-done.65.refs_1_
  368.3 2.6 collective-permute-done.67.refs_3_
  378.6 12.8 %collective-permute-done.52 = bf16[128,1024]{1,0:T(8,128)(2,1)S(1)} collective-permute-done((bf16[128,1024]{1,0:T(8,128)(2,1)S(1)}, bf16[128,1024]{1,0:T(8,128)(2,1)S(1)}, u32[]{:S(2)}, u32[]{:S(2)}) %collective-permute-start.52) | collective-permute-done | bytes 262176 | tf_op jit(solution)/shard_map/ppermute | solution.py:307
  394.1 6.2 %collective-permute-done.59 = bf16[128,1024]{1,0:T(8,128)(2,1)S(1)} collective-permute-done((bf16[128,1024]{1,0:T(8,128)(2,1)S(1)}, bf16[128,1024]{1,0:T(8,128)(2,1)S(1)}, u32[]{:S(2)}, u32[]{:S(2)}) %collective-permute-start.59) | collective-permute-done | bytes 262176 | tf_op jit(solution)/shard_map/ppermute | solution.py:311
  405.2 3.8 collective-permute-done.69.refs_5_
  409.7 10.6 %collective-permute-done.70.refs_6_ = bf16[256,384]{1,0:T(8,128)(2,1)} collective-permute-done((bf16[256,384]{1,0:T(8,128)(2,1)S(1)}, bf16[256,384]{1,0:T(8,128)(2,1)}, u32[]{:S(2)}, u32[]{:S(2)}) %collective-permute-start.70) | collective-permute-done | bytes 196640 | tf_op jit(solution)/shard_map/ppermute | solution.py:311
  431.7 50.8 %all-reduce.2 = (f32[5120]{0:T(1024)}, f32[7168]{0:T(1024)}) all-reduce(f32[5120]{0:T(1024)} %pad_maximum_fusion.15, f32[7168]{0:T(1024)S(1)} %pad_maximum_fusion.14), channel_id=1, replica_groups=mesh['ctx'=16,'fsdp'=2] {'ctx','fsdp'}, use_global_device_ids=true, to_apply=%region_10.11 | all-reduce | flops 12288 | bytes 98304 | tf_op jit(solution)/shard_map/psum | solution.py:876
  494.6 2.6 add_convert_fusion.2
  499.2 3.1 collective-permute-done.60
  503.7 5.9 %collective-permute-done.29 = bf16[256,1024]{1,0:T(8,128)(2,1)S(1)} collective-permute-done((bf16[256,1024]{1,0:T(8,128)(2,1)}, bf16[256,1024]{1,0:T(8,128)(2,1)S(1)}, u32[]{:S(2)}, u32[]{:S(2)}) %collective-permute-start.29) | collective-permute-done | bytes 524320 | tf_op jit(solution)/shard_map/ppermute | solution.py:307
  510.1 13.5 %collective-permute-done.89.refs_1_ = bf16[320,1024]{1,0:T(8,128)(2,1)S(1)} collective-permute-done((bf16[320,1024]{1,0:T(8,128)(2,1)}, bf16[320,1024]{1,0:T(8,128)(2,1)S(1)}, u32[]{:S(2)}, u32[]{:S(2)}) %collective-permute-start.89) | collective-permute-done | bytes 655392 | tf_op jit(solution)/shard_map/ppermute | solution.py:307
  535.2 2.9 collective-permute-done.93
  541.0 2.6 fusion.30
  543.7 3.5 broadcast_in_dim.25.refs_16_
  547.2 4.0 assemble_joint.1
  551.2 4.5 broadcast_in_dim.27.refs_4_
  557.3 4.4 broadcast_in_dim.29.refs_6_
  561.7 3.9 assemble_blobs.4
  565.7 3.3 assemble_blobs.5
  569.6 3.1 assemble_blobs.6
  576.0 2.7 assemble_blobs.7
  (527 shorter events, 211.5 us)
Async XLA Ops:
  0.7 64.1 %collective-permute-start = (bf16[256,1024]{1,0:T(8,128)(2,1)}, bf16[256,1024]{1,0:T(8,128)(2,1)}, u32[]{:S(2)}, u32[]{:S(2)}) collective-permute-start(bf16[256,1024]{1,0:T(8,128)(2,1)} %bitcast.55), channel_id=1, source_target_pairs={{0,8},{2,10},{8,16},{10,18},{16,24},{18,26},{24,28},{26,30},{28,20... | collective-permute-start | bytes 1572872 | tf_op jit(solution)/shard_map/ppermute | solution.py:307
  3.7 62.6 %collective-permute-start.1 = (bf16[256,1024]{1,0:T(8,128)(2,1)}, bf16[256,1024]{1,0:T(8,128)(2,1)}, u32[]{:S(2)}, u32[]{:S(2)}) collective-permute-start(bf16[256,1024]{1,0:T(8,128)(2,1)} %bitcast.56), channel_id=1, source_target_pairs={{8,0},{10,2},{16,8},{18,10},{24,16},{26,18},{28,24},{30,26},{20,28... | collective-permute-start | bytes 1572872 | tf_op jit(solution)/shard_map/ppermute | solution.py:311
  3.7 95.2 %collective-permute-start.8 = (bf16[256,1024]{1,0:T(8,128)(2,1)}, bf16[256,1024]{1,0:T(8,128)(2,1)}, u32[]{:S(2)}, u32[]{:S(2)}) collective-permute-start(bf16[256,1024]{1,0:T(8,128)(2,1)} %bitcast.57), channel_id=1, source_target_pairs={{0,2},{2,0},{4,6},{6,4},{8,10},{10,8},{12,14},{14,12},{16,18},{18,... | collective-permute-start | bytes 1572872 | tf_op jit(solution)/shard_map/ppermute | solution.py:315
  9.4 48.1 %collective-permute-start.16 = (bf16[1,13,512]{2,1,0:T(8,128)(2,1)S(1)}, bf16[1,13,512]{2,1,0:T(8,128)(2,1)S(1)}, u32[]{:S(2)}, u32[]{:S(2)}) collective-permute-start(bf16[1,13,512]{2,1,0:T(8,128)(2,1)S(1)} %bitcast.67), channel_id=1, source_target_pairs={{0,1},{1,0},{2,3},{3,2},{4,5},{5,4},{6,7},{7,6},{8,9},{9,8},{10,11... | collective-permute-start | bytes 39944 | tf_op jit(solution)/shard_map/ppermute | solution.py:319
  17.8 50.0 %collective-permute-start.18 = (bf16[512,256]{0,1:T(8,128)(2,1)}, bf16[512,256]{0,1:T(8,128)(2,1)}, u32[]{:S(2)}, u32[]{:S(2)}) collective-permute-start(bf16[512,256]{0,1:T(8,128)(2,1)} %pad.8), channel_id=1, source_target_pairs={{0,1},{1,0},{2,3},{3,2},{4,5},{5,4},{6,7},{7,6},{8,9},{9,8},{10,11... | collective-permute-start | bytes 786440 | tf_op jit(solution)/shard_map/ppermute | solution.py:319
  80.7 21.6 %collective-permute-start.9 = (bf16[256,1024]{1,0:T(8,128)(2,1)}, bf16[256,1024]{1,0:T(8,128)(2,1)S(1)}, u32[]{:S(2)}, u32[]{:S(2)}) collective-permute-start(bf16[256,1024]{1,0:T(8,128)(2,1)} %collective-permute-done), channel_id=1, source_target_pairs={{0,2},{2,0},{4,6},{6,4},{8,10},{10,8},{12,14},{14,12},{16,18},{18,... | collective-permute-start | bytes 1572872 | tf_op jit(solution)/shard_map/ppermute | solution.py:315
  80.8 22.8 %collective-permute-start.10 = (bf16[256,1024]{1,0:T(8,128)(2,1)}, bf16[256,1024]{1,0:T(8,128)(2,1)S(1)}, u32[]{:S(2)}, u32[]{:S(2)}) collective-permute-start(bf16[256,1024]{1,0:T(8,128)(2,1)} %collective-permute-done.1), channel_id=1, source_target_pairs={{0,2},{2,0},{4,6},{6,4},{8,10},{10,8},{12,14},{14,12},{16,18},{18,... | collective-permute-start | bytes 1572872 | tf_op jit(solution)/shard_map/ppermute | solution.py:315
  98.9 14.7 %collective-permute-start.34 = (bf16[256,1024]{1,0:T(8,128)(2,1)}, bf16[256,1024]{1,0:T(8,128)(2,1)}, u32[]{:S(2)}, u32[]{:S(2)}) collective-permute-start(bf16[256,1024]{1,0:T(8,128)(2,1)} %bitcast.17), channel_id=1, source_target_pairs={{0,8},{2,10},{8,16},{10,18},{16,24},{18,26},{24,28},{26,30},{28,20... | collective-permute-start | bytes 1572872 | tf_op jit(solution)/shard_map/ppermute | solution.py:307
  103.6 15.8 %collective-permute-start.13 = (bf16[256,1024]{1,0:T(8,128)(2,1)S(1)}, bf16[256,1024]{1,0:T(8,128)(2,1)S(1)}, u32[]{:S(2)}, u32[]{:S(2)}) collective-permute-start(bf16[256,1024]{1,0:T(8,128)(2,1)S(1)} %collective-permute-done.4), channel_id=1, source_target_pairs={{0,2},{2,0},{4,6},{6,4},{8,10},{10,8},{12,14},{14,12},{16,18},{18,... | collective-permute-start | bytes 1572872 | tf_op jit(solution)/shard_map/ppermute | solution.py:315
  104.5 16.3 %collective-permute-start.14 = (bf16[256,1024]{1,0:T(8,128)(2,1)S(1)}, bf16[256,1024]{1,0:T(8,128)(2,1)S(1)}, u32[]{:S(2)}, u32[]{:S(2)}) collective-permute-start(bf16[256,1024]{1,0:T(8,128)(2,1)S(1)} %collective-permute-done.5), channel_id=1, source_target_pairs={{0,2},{2,0},{4,6},{6,4},{8,10},{10,8},{12,14},{14,12},{16,18},{18,... | collective-permute-start | bytes 1572872 | tf_op jit(solution)/shard_map/ppermute | solution.py:315
  105.8 15.7 %collective-permute-start.15 = (bf16[256,1024]{1,0:T(8,128)(2,1)S(1)}, bf16[256,1024]{1,0:T(8,128)(2,1)S(1)}, u32[]{:S(2)}, u32[]{:S(2)}) collective-permute-start(bf16[256,1024]{1,0:T(8,128)(2,1)S(1)} %pad_maximum_fusion.4), channel_id=1, source_target_pairs={{0,2},{2,0},{4,6},{6,4},{8,10},{10,8},{12,14},{14,12},{16,18},{18,... | collective-permute-start | bytes 1572872 | tf_op jit(solution)/shard_map/ppermute | solution.py:315
  113.6 116.5 %collective-permute-start.42 = (bf16[256,1024]{1,0:T(8,128)(2,1)}, bf16[256,1024]{1,0:T(8,128)(2,1)}, u32[]{:S(2)}, u32[]{:S(2)}) collective-permute-start(bf16[256,1024]{1,0:T(8,128)(2,1)} %bitcast.17), channel_id=1, source_target_pairs={{0,2},{2,0},{4,6},{6,4},{8,10},{10,8},{12,14},{14,12},{16,18},{18,... | collective-permute-start | bytes 1572872 | tf_op jit(solution)/shard_map/ppermute | solution.py:315
  116.7 82.0 %collective-permute-start.36 = (bf16[256,1024]{1,0:T(8,128)(2,1)}, bf16[256,1024]{1,0:T(8,128)(2,1)}, u32[]{:S(2)}, u32[]{:S(2)}) collective-permute-start(bf16[256,1024]{1,0:T(8,128)(2,1)} %collective-permute-done.34), channel_id=1, source_target_pairs={{0,8},{2,10},{8,16},{10,18},{16,24},{18,26},{24,28},{26,30},{28,20... | collective-permute-start | bytes 1572872 | tf_op jit(solution)/shard_map/ppermute | solution.py:307
  119.4 80.9 %collective-permute-start.37 = (bf16[256,1024]{1,0:T(8,128)(2,1)}, bf16[256,1024]{1,0:T(8,128)(2,1)}, u32[]{:S(2)}, u32[]{:S(2)}) collective-permute-start(bf16[256,1024]{1,0:T(8,128)(2,1)} %collective-permute-done.35), channel_id=1, source_target_pairs={{8,0},{10,2},{16,8},{18,10},{24,16},{26,18},{28,24},{30,26},{20,28... | collective-permute-start | bytes 1572872 | tf_op jit(solution)/shard_map/ppermute | solution.py:311
  196.2 19.9 %collective-permute-start.24 = (bf16[512,1024]{1,0:T(8,128)(2,1)S(1)}, bf16[512,1024]{1,0:T(8,128)(2,1)S(1)}, u32[]{:S(2)}, u32[]{:S(2)}) collective-permute-start(bf16[512,1024]{1,0:T(8,128)(2,1)S(1)} %convolution_convert_fusion.3), channel_id=1, source_target_pairs={{0,2},{2,0},{4,6},{6,4},{8,10},{10,8},{12,14},{14,12},{16,18},{18,... | collective-permute-start | bytes 3145736 | tf_op jit(solution)/shard_map/ppermute | solution.py:315
  203.3 28.5 %collective-permute-start.43 = (bf16[256,1024]{1,0:T(8,128)(2,1)}, bf16[256,1024]{1,0:T(8,128)(2,1)S(1)}, u32[]{:S(2)}, u32[]{:S(2)}) collective-permute-start(bf16[256,1024]{1,0:T(8,128)(2,1)} %collective-permute-done.34), channel_id=1, source_target_pairs={{0,2},{2,0},{4,6},{6,4},{8,10},{10,8},{12,14},{14,12},{16,18},{18,... | collective-permute-start | bytes 1572872 | tf_op jit(solution)/shard_map/ppermute | solution.py:315
  212.8 19.7 %collective-permute-start.26 = (bf16[512,1024]{1,0:T(8,128)(2,1)S(1)}, bf16[512,1024]{1,0:T(8,128)(2,1)S(1)}, u32[]{:S(2)}, u32[]{:S(2)}) collective-permute-start(bf16[512,1024]{1,0:T(8,128)(2,1)S(1)} %convolution_convert_fusion.2), channel_id=1, source_target_pairs={{0,2},{2,0},{4,6},{6,4},{8,10},{10,8},{12,14},{14,12},{16,18},{18,... | collective-permute-start | bytes 3145736 | tf_op jit(solution)/shard_map/ppermute | solution.py:315
  230.1 127.9 %collective-permute-start.21 = (bf16[256,1024]{1,0:T(8,128)(2,1)}, bf16[256,1024]{1,0:T(8,128)(2,1)}, u32[]{:S(2)}, u32[]{:S(2)}) collective-permute-start(bf16[256,1024]{1,0:T(8,128)(2,1)} %convolution_convert_fusion.10), channel_id=1, source_target_pairs={{0,2},{2,0},{4,6},{6,4},{8,10},{10,8},{12,14},{14,12},{16,18},{18,... | collective-permute-start | bytes 1572872 | tf_op jit(solution)/shard_map/ppermute | solution.py:315
  235.9 89.9 %collective-permute-start.25 = (bf16[256,1024]{1,0:T(8,128)(2,1)}, bf16[256,1024]{1,0:T(8,128)(2,1)}, u32[]{:S(2)}, u32[]{:S(2)}) collective-permute-start(bf16[256,1024]{1,0:T(8,128)(2,1)} %pad_maximum_fusion.7), channel_id=1, source_target_pairs={{0,8},{2,10},{8,16},{10,18},{16,24},{18,26},{24,28},{26,30},{28,20... | collective-permute-start | bytes 1572872 | tf_op jit(solution)/shard_map/ppermute | solution.py:307
  239.5 86.3 %collective-permute-start.31 = (bf16[256,1024]{1,0:T(8,128)(2,1)}, bf16[256,1024]{1,0:T(8,128)(2,1)}, u32[]{:S(2)}, u32[]{:S(2)}) collective-permute-start(bf16[256,1024]{1,0:T(8,128)(2,1)} %pad_maximum_fusion.8), channel_id=1, source_target_pairs={{8,0},{10,2},{16,8},{18,10},{24,16},{26,18},{28,24},{30,26},{20,28... | collective-permute-start | bytes 1572872 | tf_op jit(solution)/shard_map/ppermute | solution.py:311
  328.3 33.4 %collective-permute-start.27 = (bf16[256,1024]{1,0:T(8,128)(2,1)}, bf16[256,1024]{1,0:T(8,128)(2,1)}, u32[]{:S(2)}, u32[]{:S(2)}) collective-permute-start(bf16[256,1024]{1,0:T(8,128)(2,1)} %get-tuple-element.77), channel_id=1, source_target_pairs={{0,8},{2,10},{8,16},{10,18},{16,24},{18,26},{24,28},{26,30},{28,20... | collective-permute-start | bytes 1572872 | tf_op jit(solution)/shard_map/ppermute | solution.py:307
  330.1 36.6 %collective-permute-start.32 = (bf16[256,1024]{1,0:T(8,128)(2,1)}, bf16[256,1024]{1,0:T(8,128)(2,1)}, u32[]{:S(2)}, u32[]{:S(2)}) collective-permute-start(bf16[256,1024]{1,0:T(8,128)(2,1)} %get-tuple-element.78), channel_id=1, source_target_pairs={{8,0},{10,2},{16,8},{18,10},{24,16},{26,18},{28,24},{30,26},{20,28... | collective-permute-start | bytes 1572872 | tf_op jit(solution)/shard_map/ppermute | solution.py:311
  357.2 34.2 %collective-permute-start.53 = (bf16[512,1024]{1,0:T(8,128)(2,1)}, bf16[512,1024]{1,0:T(8,128)(2,1)}, u32[]{:S(2)}, u32[]{:S(2)}) collective-permute-start(bf16[512,1024]{1,0:T(8,128)(2,1)} %convolution_convert_fusion.6), channel_id=1, source_target_pairs={{0,2},{2,0},{4,6},{6,4},{8,10},{10,8},{12,14},{14,12},{16,18},{18,... | collective-permute-start | bytes 3145736 | tf_op jit(solution)/shard_map/ppermute | solution.py:315
  367.7 34.6 %collective-permute-start.84 = (bf16[320,1024]{1,0:T(8,128)(2,1)S(1)}, bf16[320,1024]{1,0:T(8,128)(2,1)S(1)}, u32[]{:S(2)}, u32[]{:S(2)}) collective-permute-start(bf16[320,1024]{1,0:T(8,128)(2,1)S(1)} %maximum_maximum_fusion.refs_0_), channel_id=1, source_target_pairs={{8,0},{10,2},{16,8},{18,10},{24,16},{26,18},{28,24},{30,26},{20,28... | collective-permute-start | bytes 1966088 | tf_op jit(solution)/shard_map/ppermute | solution.py:311
  370.9 32.9 %collective-permute-start.87 = (bf16[320,1024]{1,0:T(8,128)(2,1)S(1)}, bf16[320,1024]{1,0:T(8,128)(2,1)}, u32[]{:S(2)}, u32[]{:S(2)}) collective-permute-start(bf16[320,1024]{1,0:T(8,128)(2,1)S(1)} %maximum_maximum_fusion.refs_0_), channel_id=1, source_target_pairs={{0,8},{2,10},{8,16},{10,18},{16,24},{18,26},{24,28},{26,30},{28,20... | collective-permute-start | bytes 1966088 | tf_op jit(solution)/shard_map/ppermute | solution.py:307
  374.4 29.4 %collective-permute-start.96 = (bf16[320,1024]{1,0:T(8,128)(2,1)S(1)}, bf16[320,1024]{1,0:T(8,128)(2,1)S(1)}, u32[]{:S(2)}, u32[]{:S(2)}) collective-permute-start(bf16[320,1024]{1,0:T(8,128)(2,1)S(1)} %maximum_maximum_fusion.refs_0_), channel_id=1, source_target_pairs={{0,2},{2,0},{4,6},{6,4},{8,10},{10,8},{12,14},{14,12},{16,18},{18,... | collective-permute-start | bytes 1966088 | tf_op jit(solution)/shard_map/ppermute | solution.py:315
  375.1 16.3 %collective-permute-start.52 = (bf16[128,1024]{1,0:T(8,128)(2,1)S(1)}, bf16[128,1024]{1,0:T(8,128)(2,1)S(1)}, u32[]{:S(2)}, u32[]{:S(2)}) collective-permute-start(bf16[128,1024]{1,0:T(8,128)(2,1)S(1)} %get-tuple-element.85), channel_id=1, source_target_pairs={{0,8},{2,10},{8,16},{10,18},{16,24},{18,26},{24,28},{26,30},{28,20... | collective-permute-start | bytes 786440 | tf_op jit(solution)/shard_map/ppermute | solution.py:307
  391.4 37.9 %collective-permute-start.55 = (bf16[512,1024]{1,0:T(8,128)(2,1)}, bf16[512,1024]{1,0:T(8,128)(2,1)}, u32[]{:S(2)}, u32[]{:S(2)}) collective-permute-start(bf16[512,1024]{1,0:T(8,128)(2,1)} %convolution_convert_fusion.5), channel_id=1, source_target_pairs={{0,2},{2,0},{4,6},{6,4},{8,10},{10,8},{12,14},{14,12},{16,18},{18,... | collective-permute-start | bytes 3145736 | tf_op jit(solution)/shard_map/ppermute | solution.py:315
  401.8 27.5 %collective-permute-start.33 = (bf16[256,1024]{1,0:T(8,128)(2,1)}, bf16[256,1024]{1,0:T(8,128)(2,1)}, u32[]{:S(2)}, u32[]{:S(2)}) collective-permute-start(bf16[256,1024]{1,0:T(8,128)(2,1)} %get-tuple-element.76), channel_id=1, source_target_pairs={{8,0},{10,2},{16,8},{18,10},{24,16},{26,18},{28,24},{30,26},{20,28... | collective-permute-start | bytes 1572872 | tf_op jit(solution)/shard_map/ppermute | solution.py:311
  403.8 19.0 %collective-permute-start.76 = (bf16[256,384]{1,0:T(8,128)(2,1)S(1)}, bf16[256,384]{1,0:T(8,128)(2,1)S(1)}, u32[]{:S(2)}, u32[]{:S(2)}) collective-permute-start(bf16[256,384]{1,0:T(8,128)(2,1)S(1)} %collective-permute-done.67.refs_3_), channel_id=1, source_target_pairs={{0,2},{2,0},{4,6},{6,4},{8,10},{10,8},{12,14},{14,12},{16,18},{18,... | collective-permute-start | bytes 589832 | tf_op jit(solution)/shard_map/ppermute | solution.py:315
  403.8 16.4 %collective-permute-start.70 = (bf16[256,384]{1,0:T(8,128)(2,1)S(1)}, bf16[256,384]{1,0:T(8,128)(2,1)}, u32[]{:S(2)}, u32[]{:S(2)}) collective-permute-start(bf16[256,384]{1,0:T(8,128)(2,1)S(1)} %collective-permute-done.68.refs_4_), channel_id=1, source_target_pairs={{8,0},{10,2},{16,8},{18,10},{24,16},{26,18},{28,24},{30,26},{20,28... | collective-permute-start | bytes 589832 | tf_op jit(solution)/shard_map/ppermute | solution.py:311
  409.0 17.2 %collective-permute-start.77 = (bf16[256,384]{1,0:T(8,128)(2,1)S(1)}, bf16[256,384]{1,0:T(8,128)(2,1)S(1)}, u32[]{:S(2)}, u32[]{:S(2)}) collective-permute-start(bf16[256,384]{1,0:T(8,128)(2,1)S(1)} %collective-permute-done.68.refs_4_), channel_id=1, source_target_pairs={{0,2},{2,0},{4,6},{6,4},{8,10},{10,8},{12,14},{14,12},{16,18},{18,... | collective-permute-start | bytes 589832 | tf_op jit(solution)/shard_map/ppermute | solution.py:315
  420.3 74.3 %collective-permute-start.88 = (bf16[320,1024]{1,0:T(8,128)(2,1)}, bf16[320,1024]{1,0:T(8,128)(2,1)}, u32[]{:S(2)}, u32[]{:S(2)}) collective-permute-start(bf16[320,1024]{1,0:T(8,128)(2,1)} %collective-permute-done.87.refs_1_), channel_id=1, source_target_pairs={{0,8},{2,10},{8,16},{10,18},{16,24},{18,26},{24,28},{26,30},{28,20... | collective-permute-start | bytes 1966088 | tf_op jit(solution)/shard_map/ppermute | solution.py:307
  423.5 70.9 %collective-permute-start.54 = (bf16[256,1024]{1,0:T(8,128)(2,1)}, bf16[256,1024]{1,0:T(8,128)(2,1)}, u32[]{:S(2)}, u32[]{:S(2)}) collective-permute-start(bf16[256,1024]{1,0:T(8,128)(2,1)} %pad_maximum_fusion.10), channel_id=1, source_target_pairs={{0,8},{2,10},{8,16},{10,18},{16,24},{18,26},{24,28},{26,30},{28,20... | collective-permute-start | bytes 1572872 | tf_op jit(solution)/shard_map/ppermute | solution.py:307
  426.9 70.3 %collective-permute-start.85 = (bf16[320,1024]{1,0:T(8,128)(2,1)S(1)}, bf16[320,1024]{1,0:T(8,128)(2,1)}, u32[]{:S(2)}, u32[]{:S(2)}) collective-permute-start(bf16[320,1024]{1,0:T(8,128)(2,1)S(1)} %collective-permute-done.84.refs_2_), channel_id=1, source_target_pairs={{8,0},{10,2},{16,8},{18,10},{24,16},{26,18},{28,24},{30,26},{20,28... | collective-permute-start | bytes 1966088 | tf_op jit(solution)/shard_map/ppermute | solution.py:311
  429.2 80.4 %collective-permute-start.57 = (bf16[512,1024]{1,0:T(8,128)(2,1)}, bf16[512,1024]{1,0:T(8,128)(2,1)}, u32[]{:S(2)}, u32[]{:S(2)}) collective-permute-start(bf16[512,1024]{1,0:T(8,128)(2,1)} %convolution_convert_fusion.4), channel_id=1, source_target_pairs={{0,2},{2,0},{4,6},{6,4},{8,10},{10,8},{12,14},{14,12},{16,18},{18,... | collective-permute-start | bytes 3145736 | tf_op jit(solution)/shard_map/ppermute | solution.py:315
  429.2 54.2 %collective-permute-start.71 = (bf16[128,384]{1,0:T(8,128)(2,1)}, bf16[128,384]{1,0:T(8,128)(2,1)S(1)}, u32[]{:S(2)}, u32[]{:S(2)}) collective-permute-start(bf16[128,384]{1,0:T(8,128)(2,1)} %slice.337), channel_id=1, source_target_pairs={{0,8},{2,10},{8,16},{10,18},{16,24},{18,26},{24,28},{26,30},{28,20... | collective-permute-start | bytes 294920 | tf_op jit(solution)/shard_map/ppermute | solution.py:307
  494.5 15.1 %collective-permute-start.29 = (bf16[256,1024]{1,0:T(8,128)(2,1)}, bf16[256,1024]{1,0:T(8,128)(2,1)S(1)}, u32[]{:S(2)}, u32[]{:S(2)}) collective-permute-start(bf16[256,1024]{1,0:T(8,128)(2,1)} %get-tuple-element.75), channel_id=1, source_target_pairs={{0,8},{2,10},{8,16},{10,18},{16,24},{18,26},{24,28},{26,30},{28,20... | collective-permute-start | bytes 1572872 | tf_op jit(solution)/shard_map/ppermute | solution.py:307
  494.5 29.1 %collective-permute-start.89 = (bf16[320,1024]{1,0:T(8,128)(2,1)}, bf16[320,1024]{1,0:T(8,128)(2,1)S(1)}, u32[]{:S(2)}, u32[]{:S(2)}) collective-permute-start(bf16[320,1024]{1,0:T(8,128)(2,1)} %collective-permute-done.88.refs_3_), channel_id=1, source_target_pairs={{0,8},{2,10},{8,16},{10,18},{16,24},{18,26},{24,28},{26,30},{28,20... | collective-permute-start | bytes 1966088 | tf_op jit(solution)/shard_map/ppermute | solution.py:307
  497.2 27.9 %collective-permute-start.91 = (bf16[320,1024]{1,0:T(8,128)(2,1)}, bf16[320,1024]{1,0:T(8,128)(2,1)S(1)}, u32[]{:S(2)}, u32[]{:S(2)}) collective-permute-start(bf16[320,1024]{1,0:T(8,128)(2,1)} %collective-permute-done.85.refs_0_), channel_id=1, source_target_pairs={{8,0},{10,2},{16,8},{18,10},{24,16},{26,18},{28,24},{30,26},{20,28... | collective-permute-start | bytes 1966088 | tf_op jit(solution)/shard_map/ppermute | solution.py:311
  509.6 16.9 %collective-permute-start.79 = (bf16[256,384]{1,0:T(8,128)(2,1)}, bf16[256,384]{1,0:T(8,128)(2,1)S(1)}, u32[]{:S(2)}, u32[]{:S(2)}) collective-permute-start(bf16[256,384]{1,0:T(8,128)(2,1)} %collective-permute-done.70.refs_6_), channel_id=1, source_target_pairs={{0,2},{2,0},{4,6},{6,4},{8,10},{10,8},{12,14},{14,12},{16,18},{18,... | collective-permute-start | bytes 589832 | tf_op jit(solution)/shard_map/ppermute | solution.py:315
  509.6 18.9 %collective-permute-start.80 = (bf16[256,384]{1,0:T(8,128)(2,1)S(1)}, bf16[256,384]{1,0:T(8,128)(2,1)S(1)}, u32[]{:S(2)}, u32[]{:S(2)}) collective-permute-start(bf16[256,384]{1,0:T(8,128)(2,1)S(1)} %constant_dynamic-update-slice_fusion.34.refs_7_), channel_id=1, source_target_pairs={{0,2},{2,0},{4,6},{6,4},{8,10},{10,8},{12,14},{14,12},{16,18},{18,... | collective-permute-start | bytes 589832 | tf_op jit(solution)/shard_map/ppermute | solution.py:315
  510.1 22.4 %collective-permute-start.56 = (bf16[256,1024]{1,0:T(8,128)(2,1)S(1)}, bf16[256,1024]{1,0:T(8,128)(2,1)S(1)}, u32[]{:S(2)}, u32[]{:S(2)}) collective-permute-start(bf16[256,1024]{1,0:T(8,128)(2,1)S(1)} %get-tuple-element.69), channel_id=1, source_target_pairs={{0,8},{2,10},{8,16},{10,18},{16,24},{18,26},{24,28},{26,30},{28,20... | collective-permute-start | bytes 1572872 | tf_op jit(solution)/shard_map/ppermute | solution.py:307
  532.5 36.4 %collective-permute-start.98 = (bf16[320,1024]{1,0:T(8,128)(2,1)S(1)}, bf16[320,1024]{1,0:T(8,128)(2,1)S(1)}, u32[]{:S(2)}, u32[]{:S(2)}) collective-permute-start(bf16[320,1024]{1,0:T(8,128)(2,1)S(1)} %collective-permute-done.84.refs_2_), channel_id=1, source_target_pairs={{0,2},{2,0},{4,6},{6,4},{8,10},{10,8},{12,14},{14,12},{16,18},{18,... | collective-permute-start | bytes 1966088 | tf_op jit(solution)/shard_map/ppermute | solution.py:315
  534.2 34.8 %collective-permute-start.99 = (bf16[320,1024]{1,0:T(8,128)(2,1)}, bf16[320,1024]{1,0:T(8,128)(2,1)S(1)}, u32[]{:S(2)}, u32[]{:S(2)}) collective-permute-start(bf16[320,1024]{1,0:T(8,128)(2,1)} %collective-permute-done.88.refs_3_), channel_id=1, source_target_pairs={{0,2},{2,0},{4,6},{6,4},{8,10},{10,8},{12,14},{14,12},{16,18},{18,... | collective-permute-start | bytes 1966088 | tf_op jit(solution)/shard_map/ppermute | solution.py:315
  534.6 38.0 %collective-permute-start.50 = (bf16[256,1024]{1,0:T(8,128)(2,1)}, bf16[256,1024]{1,0:T(8,128)(2,1)S(1)}, u32[]{:S(2)}, u32[]{:S(2)}) collective-permute-start(bf16[256,1024]{1,0:T(8,128)(2,1)} %convolution_convert_fusion.8), channel_id=1, source_target_pairs={{0,2},{2,0},{4,6},{6,4},{8,10},{10,8},{12,14},{14,12},{16,18},{18,... | collective-permute-start | bytes 1572872 | tf_op jit(solution)/shard_map/ppermute | solution.py:315
  538.1 34.6 %collective-permute-start.62 = (bf16[256,1024]{1,0:T(8,128)(2,1)S(1)}, bf16[256,1024]{1,0:T(8,128)(2,1)S(1)}, u32[]{:S(2)}, u32[]{:S(2)}) collective-permute-start(bf16[256,1024]{1,0:T(8,128)(2,1)S(1)} %get-tuple-element.68), channel_id=1, source_target_pairs={{8,0},{10,2},{16,8},{18,10},{24,16},{26,18},{28,24},{30,26},{20,28... | collective-permute-start | bytes 1572872 | tf_op jit(solution)/shard_map/ppermute | solution.py:311
  540.2 33.0 %collective-permute-start.58 = (bf16[256,1024]{1,0:T(8,128)(2,1)S(1)}, bf16[256,1024]{1,0:T(8,128)(2,1)S(1)}, u32[]{:S(2)}, u32[]{:S(2)}) collective-permute-start(bf16[256,1024]{1,0:T(8,128)(2,1)S(1)} %get-tuple-element.67), channel_id=1, source_target_pairs={{0,8},{2,10},{8,16},{10,18},{16,24},{18,26},{24,28},{26,30},{28,20... | collective-permute-start | bytes 1572872 | tf_op jit(solution)/shard_map/ppermute | solution.py:307
  (136 other events, 2185.5 us)

commit v2 on v0

--- a/solution.py
+++ b/solution.py
@@ -1,6 +1,10 @@
+import functools
+
 import jax
 import jax.numpy as jnp
 from jax import lax
+from jax.experimental import pallas as pl
+from jax.experimental.pallas import tpu as pltpu
 from jax.sharding import PartitionSpec as P
 
 HEADS = 16
@@ -288,10 +292,858 @@
         column_total,
     )
 
+CYCLE = (0, 2, 4, 6, 7, 5, 3, 1)
+RING = tuple((2 * CYCLE[i], 2 * CYCLE[(i + 1) % 8]) for i in range(8)) + tuple(
+    (2 * CYCLE[i] + 1, 2 * CYCLE[i - 1] + 1) for i in range(8)
+)
+SWAP = tuple((i, i ^ 1) for i in range(16))
+TILE = 512
+BLOCK = 128
+MIB = 1024 * 1024
+
+
+def hop(values):
+    return lax.ppermute(values, "ctx", RING)
+
+
+def swap(values):
+    return lax.ppermute(values, "ctx", SWAP)
+
+
+def other(values):
+    return lax.ppermute(values, "fsdp", ((0, 1), (1, 0)))
+
+
+def after(values, *others):
+    return lax.optimization_barrier((values, *others))[0]
+
+
+def cut(values, start, size, axis):
+    return lax.dynamic_slice_in_dim(values, start, size, axis)
+
+
+def ring_gather(own, core, gates=(None, None, None, None)):
+    size = own.shape[0]
+    partner = swap(own)
+    pair = jnp.where(
+        core == 0, jnp.concatenate([own, partner], 0), jnp.concatenate([partner, own], 0)
+    )
+    blocks, hops = [pair], []
+    held = pair
+    for step in range(3):
+        if gates[step] is not None:
+            held = after(held, gates[step])
+        held = hop(held)
+        hops.append(held)
+        blocks += [held, swap(held)]
+    far = cut(held, core * size, size, 0)
+    if gates[3] is not None:
+        far = after(far, gates[3])
+    far = hop(far)
+    hops.append(far)
+    blocks.append(jnp.concatenate([far, swap(far)], 0))
+    return blocks, hops
+
+
+def piece_owners(me):
+    core = me % 2
+    cycle = jnp.array(CYCLE, jnp.int32)
+    place = jnp.array([CYCLE.index(i) for i in range(8)], jnp.int32)[me // 2]
+    toward = 2 * core - 1
+    steps = jnp.array([0, 1, -1, 2, -2, 3, -3], jnp.int32) * toward
+    chips = cycle[(place + steps) % 8]
+    pairs = (2 * chips[:, None] + jnp.arange(2, dtype=jnp.int32)[None, :]).reshape(-1)
+    far = cycle[(place + 4) % 8]
+    return jnp.concatenate([pairs, jnp.stack([2 * far + core, 2 * far + 1 - core])]).astype(
+        jnp.int32
+    )
+
+
+def ring_scatter(values, weight, core, gates=(None, None, None, None)):
+    rows = values.shape[0] // 16
+    f32, bf16 = jnp.float32, jnp.bfloat16
+
+    def term(first, count):
+        return nn(values[first * rows : (first + count) * rows], weight)
+
+    def gated(held, step):
+        return held if gates[step] is None else after(held, gates[step])
+
+    far = (term(14, 1) + swap(term(15, 1).astype(bf16)).astype(f32)).astype(bf16)
+    held = hop(gated(far, 0))
+    hops = [held]
+    for step in (3, 2, 1):
+        theirs = swap(term(4 * step - 2, 2).astype(bf16))
+        mine = term(4 * step, 2) + theirs.astype(f32)
+        if step == 3:
+            blank = jnp.zeros_like(held)
+            held = jnp.where(
+                core == 0,
+                jnp.concatenate([held, blank], 0),
+                jnp.concatenate([blank, held], 0),
+            )
+        held = hop(gated((mine + held.astype(f32)).astype(bf16), 4 - step))
+        hops.append(held)
+    total = term(0, 2) + held.astype(f32)
+    sent = cut(total, (1 - core) * rows, rows, 0).astype(bf16)
+    return cut(total, core * rows, rows, 0) + swap(sent).astype(f32), hops
+
+
+def turn_back(values, lanes):
+    ahead = pltpu.roll(values, 128 - ROT // 2, 1)
+    behind = pltpu.roll(values, ROT // 2, 1)
+    return jnp.where(lanes % 64 < ROT // 2, -ahead, behind)
+
+
+def nt(left_side, right_side):
+    return lax.dot_general(
+        left_side, right_side, (((1,), (1,)), ((), ())), preferred_element_type=jnp.float32
+    )
+
+
+def nn(left_side, right_side):
+    return jnp.dot(left_side, right_side, preferred_element_type=jnp.float32)
+
+
+def tn(left_side, right_side):
+    return lax.dot_general(
+        left_side, right_side, (((0,), (0,)), ((), ())), preferred_element_type=jnp.float32
+    )
+
+
+VMEM = pl.BlockSpec(memory_space=pltpu.VMEM)
+SMEM = pl.BlockSpec(memory_space=pltpu.SMEM)
+ANY = pl.BlockSpec(memory_space=pl.ANY)
+
+
+def shaped(shape, dtype):
+    return jax.ShapeDtypeStruct(shape, dtype)
+
+
+def pre_kernel(x, norms, joint_w, joint_b, expand_w, expand_b, *refs):
+    one, two, joint, active, slope = refs[-5:]
+    wide = x[...].astype(jnp.float32)
+    center = wide - jnp.mean(wide, -1, keepdims=True)
+    spread = jnp.mean(center * center, -1, keepdims=True)
+    unit = center * lax.rsqrt(spread + epsilon)
+    normed_one = (unit * norms[0:1, :] + norms[1:2, :]).astype(jnp.bfloat16)
+    normed_two = (unit * norms[2:3, :] + norms[3:4, :]).astype(jnp.bfloat16)
+    one[...] = normed_one
+    two[...] = normed_two
+    joint[...] = nn(normed_one, joint_w[...]) + joint_b[...]
+    expanded = nn(normed_two, expand_w[...]) + expand_b[...]
+    share = 0.5 + 0.5 * lax.erf(expanded * (0.5**0.5))
+    active[...] = (expanded * share).astype(jnp.bfloat16)
+    slope[...] = share + expanded * (jnp.exp(-0.5 * expanded * expanded) * 0.3989422804014327)
+
+
+def pre(index, x, norms, joint_w, joint_b, expand_w, expand_b, outs, count):
+    rows, width = x.shape
+    step = rows // 2
+    fixed = lambda shape: pl.BlockSpec(shape, lambda i: (0, 0))
+    place = lambda cols: pl.BlockSpec((step, cols), lambda i: (2 * index + i, 0))
+    total = rows * count
+    bf16, f32 = jnp.bfloat16, jnp.float32
+    aliases = {} if outs is None else {6 + i: i for i in range(5)}
+    return pl.pallas_call(
+        pre_kernel,
+        grid=(2,),
+        in_specs=[pl.BlockSpec((step, width), lambda i: (i, 0))]
+        + [fixed(v.shape) for v in (norms, joint_w, joint_b, expand_w, expand_b)]
+        + [ANY] * len(aliases),
+        out_specs=[place(width), place(width), place(256), place(256), place(256)],
+        out_shape=[
+            shaped((total, width), bf16),
+            shaped((total, width), bf16),
+            shaped((total, 256), f32),
+            shaped((total, 256), bf16),
+            shaped((total, 256), f32),
+        ],
+        input_output_aliases=aliases,
+        compiler_params=pltpu.CompilerParams(vmem_limit_bytes=40 * MIB),
+        cost_estimate=pl.CostEstimate(
+            flops=rows * width * 1024, bytes_accessed=rows * width * 10, transcendentals=rows * 512
+        ),
+        name="norms_joint_hidden",
+    )(x, norms, joint_w, joint_b, expand_w, expand_b, *(outs or ()))
+
+
+def tables(angle_rows):
+    lanes = jnp.arange(128) % 64
+    inverse = jnp.power(10000.0, -2.0 * (lanes % (ROT // 2)).astype(jnp.float32) / ROT)
+    angles = angle_rows.astype(jnp.float32)[:, None] * jnp.where(lanes < ROT, inverse, 0.0)[None, :]
+    return jnp.cos(angles), jnp.sin(angles)
+
+
+def turn_kernel(blocks, joint, cos_far, sin_far, cos_near, sin_near, q_out, k_out, v_out):
+    rows = joint.shape[0]
+    lanes = lax.broadcasted_iota(jnp.int32, (BLOCK, 128), 1)
+
+    def sort(s, _):
+        p = blocks[s]
+        source = pl.ds(pl.multiple_of(s * BLOCK, BLOCK), BLOCK)
+        target = pl.ds(pl.multiple_of(p * BLOCK, BLOCK), BLOCK)
+        far = pl.ds(p, 1)
+        cosine = cos_far[far, :] * cos_near[...] - sin_far[far, :] * sin_near[...]
+        sine = sin_far[far, :] * cos_near[...] + cos_far[far, :] * sin_near[...]
+        pair = joint[source, 0:128]
+        pair = pair * cosine + turn_back(pair, lanes) * sine
+        q_out[target, :] = pair[:, 0:64].astype(jnp.bfloat16)
+        k_out[target, :] = pair[:, 64:128].astype(jnp.bfloat16)
+        v_out[target, :] = joint[source, 128:192].astype(jnp.bfloat16)
+        return 0
+
+    lax.fori_loop(0, rows // BLOCK, sort, 0)
+
+
+def turn(blocks, joint, angles):
+    rows = joint.shape[0]
+    head = shaped((rows, 64), jnp.bfloat16)
+    return pl.pallas_call(
+        turn_kernel,
+        in_specs=[SMEM] + [VMEM] * 5,
+        out_specs=[VMEM] * 3,
+        out_shape=[head] * 3,
+        compiler_params=pltpu.CompilerParams(vmem_limit_bytes=40 * MIB),
+        cost_estimate=pl.CostEstimate(flops=0, bytes_accessed=rows * 2048, transcendentals=0),
+        name="rotary_and_sort",
+    )(blocks, joint, *angles)
+
+
+def below_diagonal():
+    return lax.broadcasted_iota(jnp.int32, (TILE, TILE), 0) <= lax.broadcasted_iota(
+        jnp.int32, (TILE, TILE), 1
+    )
+
+
+def forward_kernel(index, slots, q, k, v, *refs):
+    mixed_out, out, lse = refs[-5:-2]
+    buffer, sems = refs[-2:]
+    tiles = q.shape[0] // TILE
+    below = below_diagonal()
+    parts = TILE // BLOCK
+    copies = []
+    for which, i in enumerate((index, tiles - 1 - index)):
+        query = q[i * TILE : (i + 1) * TILE, :] * jnp.bfloat16(0.125)
+
+        def step(j, carry, masked):
+            top, total, acc = carry
+            there = pl.ds(pl.multiple_of(j * TILE, TILE), TILE)
+            scores = nt(k[there, :], query)
+            if masked:
+                scores = jnp.where(below, scores, negative)
+            new_top = jnp.maximum(top, jnp.max(scores, 0, keepdims=True))
+            weights = jnp.exp(scores - new_top)
+            keep = jnp.exp(top - new_top)
+            total = total * keep + jnp.sum(weights, 0, keepdims=True)
+            return new_top, total, acc * keep + tn(v[there, :], weights.astype(jnp.bfloat16))
+
+        carry = (
+            jnp.full((1, TILE), negative, jnp.float32),
+            jnp.zeros((1, TILE), jnp.float32),
+            jnp.zeros((64, TILE), jnp.float32),
+        )
+        carry = lax.fori_loop(0, i, lambda j, c: step(j, c, False), carry)
+        top, total, acc = step(i, carry, True)
+        acc = acc / total
+        here = slice(which * TILE, (which + 1) * TILE)
+        out[:, here] = acc
+        lse[:, here] = top + jnp.log(total)
+        buffer[here, :] = acc.T.astype(jnp.bfloat16)
+        for part in range(parts):
+            slot = slots[i * parts + part]
+            copies.append(
+                pltpu.make_async_copy(
+                    buffer.at[pl.ds(which * TILE + part * BLOCK, BLOCK)],
+                    mixed_out.at[pl.ds(pl.multiple_of(slot * BLOCK, BLOCK), BLOCK)],
+                    sems.at[which * parts + part],
+                )
+            )
+            copies[-1].start()
+    for copy in copies:
+        copy.wait()
+
+
+def attention_forward(index, slots, q, k, v, mixed, gate):
+    rows = q.shape[0]
+    extra = ([] if mixed is None else [mixed]) + ([] if gate is None else [gate])
+    return pl.pallas_call(
+        functools.partial(forward_kernel, index),
+        in_specs=[SMEM] + [VMEM] * 3 + [ANY] * len(extra),
+        out_specs=[ANY, VMEM, VMEM],
+        out_shape=[
+            shaped((rows, 64), jnp.bfloat16),
+            shaped((64, 2 * TILE), jnp.float32),
+            shaped((1, 2 * TILE), jnp.float32),
+        ],
+        scratch_shapes=[
+            pltpu.VMEM((2 * TILE, 64), jnp.bfloat16),
+            pltpu.SemaphoreType.DMA((2 * TILE // BLOCK,)),
+        ],
+        input_output_aliases={} if mixed is None else {4: 0},
+        compiler_params=pltpu.CompilerParams(vmem_limit_bytes=40 * MIB),
+        cost_estimate=pl.CostEstimate(
+            flops=rows * rows * 256, bytes_accessed=rows * 1024, transcendentals=rows * rows // 8
+        ),
+        name="attention_forward",
+    )(slots, q, k, v, *extra)
+
+
+def post_kernel(pieces, *refs):
+    blocks = refs[:pieces]
+    slope, active, mixed, shrink, dense = refs[pieces : pieces + 5]
+    delta, mixed_grad, shrink_grad, dense_grad, column, delta_sum, held = refs[pieces + 5 :]
+    step = pl.program_id(0)
+    for n in range(pieces):
+
+        @pl.when(step == n)
+        def _(n=n):
+            held[...] = blocks[n][...]
+
+    @pl.when(step == 0)
+    def _():
+        shrink_grad[...] = jnp.zeros_like(shrink_grad)
+        dense_grad[...] = jnp.zeros_like(dense_grad)
+        column[...] = jnp.zeros_like(column)
+        delta_sum[...] = jnp.zeros_like(delta_sum)
+
+    grad = held[...]
+    column[...] += jnp.sum(grad.astype(jnp.float32), 0, keepdims=True)
+    rounded = (nt(grad, shrink[...]) * slope[...]).astype(jnp.bfloat16)
+    delta[...] = rounded
+    delta_sum[...] += jnp.sum(rounded.astype(jnp.float32), 0, keepdims=True)
+    mixed_grad[...] = nt(grad, dense[...]).astype(jnp.bfloat16)
+    shrink_grad[...] += tn(active[...], grad)
+    dense_grad[...] += tn(mixed[...], grad)
+
+
+def post(blocks, slope, active, mixed, shrink, dense):
+    count = len(blocks)
+    rows, width = blocks[0].shape
+    total = rows * count
+    row = lambda cols: pl.BlockSpec((rows, cols), lambda i: (i, 0))
+    fixed = lambda shape: pl.BlockSpec(shape, lambda i: (0, 0))
+    f32, bf16 = jnp.float32, jnp.bfloat16
+    return pl.pallas_call(
+        functools.partial(post_kernel, count),
+        grid=(count,),
+        in_specs=[VMEM] * count
+        + [row(256), row(256), row(64), fixed(shrink.shape), fixed(dense.shape)],
+        out_specs=[
+            row(256),
+            row(64),
+            fixed((256, width)),
+            fixed((64, width)),
+            fixed((1, width)),
+            fixed((1, 256)),
+        ],
+        out_shape=[
+            shaped((total, 256), bf16),
+            shaped((total, 64), bf16),
+            shaped((256, width), f32),
+            shaped((64, width), f32),
+            shaped((1, width), f32),
+            shaped((1, 256), f32),
+        ],
+        scratch_shapes=[pltpu.VMEM((rows, width), bf16)],
+        compiler_params=pltpu.CompilerParams(vmem_limit_bytes=44 * MIB),
+        cost_estimate=pl.CostEstimate(
+            flops=total * width * 1280, bytes_accessed=total * width * 4, transcendentals=0
+        ),
+        name="cotangent_products",
+    )(*blocks, slope, active, mixed, shrink, dense)
+
+
+def sort_grad_kernel(tiles, slots, mixed_grad, *refs):
+    outs = refs[:tiles]
+    grad, inner = refs[-2:]
+    per_tile = TILE // BLOCK
+
+    for p in range(slots.shape[0]):
+        tile, part = divmod(p, per_tile)
+        column = part * BLOCK
+        if tile >= tiles:
+            tile, column = 2 * tiles - 1 - tile, column + TILE
+        source = pl.ds(pl.multiple_of(slots[p] * BLOCK, BLOCK), BLOCK)
+        piece = mixed_grad[source, :]
+        here = slice(p * BLOCK, (p + 1) * BLOCK)
+        grad[here, :] = piece
+        flat = piece.astype(jnp.float32).T
+        inner[:, here] = jnp.sum(
+            flat * outs[tile][:, column : column + BLOCK], 0, keepdims=True
+        )
+
+
+def sort_grad(slots, mixed_grad, outs):
+    rows = mixed_grad.shape[0]
+    return pl.pallas_call(
+        functools.partial(sort_grad_kernel, len(outs)),
+        in_specs=[SMEM] + [VMEM] * (1 + len(outs)),
+        out_specs=[VMEM] * 2,
+        out_shape=[shaped((rows, 64), jnp.bfloat16), shaped((1, rows), jnp.float32)],
+        compiler_params=pltpu.CompilerParams(vmem_limit_bytes=40 * MIB),
+        cost_estimate=pl.CostEstimate(flops=0, bytes_accessed=rows * 1024, transcendentals=0),
+        name="sort_gradient",
+    )(slots, mixed_grad, *outs)
+
+
+def backward_kernel(index, first, q, k, v, grad, inner, lse, *refs):
+    dq, dk, dv = refs[-3:]
+    tiles = q.shape[0] // TILE
+    below = below_diagonal()
+    if first:
+        dq[...] = jnp.zeros_like(dq)
+    else:
+        dq[...] = refs[0][...]
+    for which, j in enumerate((index, tiles - 1 - index)):
+        key = k[j * TILE : (j + 1) * TILE, :]
+        value = v[j * TILE : (j + 1) * TILE, :]
+
+        def step(i, carry, masked):
+            key_grad, value_grad = carry
+            here = pl.ds(pl.multiple_of(i * TILE, TILE), TILE)
+            query = q[here, :] * jnp.bfloat16(0.125)
+            out_grad = grad[here, :]
+            probs = jnp.exp(nt(key, query) - lse[:, here])
+            if masked:
+                probs = jnp.where(below, probs, 0.0)
+            score_grad = (probs * (nt(value, out_grad) - inner[:, here])).astype(jnp.bfloat16)
+            value_grad = value_grad + nn(probs.astype(jnp.bfloat16), out_grad)
+            key_grad = key_grad + nn(score_grad, query)
+            dq[:, here] += tn(key, score_grad)
+            return key_grad, value_grad
+
+        zero = jnp.zeros((TILE, 64), jnp.float32)
+        carry = step(j, (zero, zero), True)
+        key_grad, value_grad = lax.fori_loop(
+            j + 1, tiles, lambda i, c: step(i, c, False), carry
+        )
+        here = slice(which * TILE, (which + 1) * TILE)
+        dk[here, :] = key_grad
+        dv[here, :] = value_grad
+
+
+def attention_backward(index, q, k, v, grad, inner, lse, dq, gate):
+    rows = q.shape[0]
+    extra = ([] if dq is None else [dq]) + ([] if gate is None else [gate])
+    specs = ([] if dq is None else [VMEM]) + ([] if gate is None else [ANY])
+    return pl.pallas_call(
+        functools.partial(backward_kernel, index, dq is None),
+        in_specs=[VMEM] * 6 + specs,
+        out_specs=[VMEM] * 3,
+        out_shape=[
+            shaped((64, rows), jnp.float32),
+            shaped((2 * TILE, 64), jnp.float32),
+            shaped((2 * TILE, 64), jnp.float32),
+        ],
+        compiler_params=pltpu.CompilerParams(vmem_limit_bytes=40 * MIB),
+        cost_estimate=pl.CostEstimate(
+            flops=rows * rows * 640, bytes_accessed=rows * 2048, transcendentals=rows * rows // 8
+        ),
+        name="attention_backward",
+    )(q, k, v, grad, inner, lse, *extra)
+
+
+def finish_kernel(tiles, slots, dq, cos_far, sin_far, cos_near, sin_near, *refs):
+    key_grads, value_grads = refs[:tiles], refs[tiles : 2 * tiles]
+    delta, total = refs[-2:]
+    lanes = lax.broadcasted_iota(jnp.int32, (BLOCK, 128), 1)
+    per_tile = TILE // BLOCK
+    total[...] = jnp.zeros_like(total)
+    for p in range(slots.shape[0]):
+        tile, part = divmod(p, per_tile)
+        row = part * BLOCK
+        if tile >= tiles:
+            tile, row = 2 * tiles - 1 - tile, row + TILE
+        target = pl.ds(pl.multiple_of(slots[p] * BLOCK, BLOCK), BLOCK)
+        cosine = cos_far[p : p + 1, :] * cos_near[...] - sin_far[p : p + 1, :] * sin_near[...]
+        sine = sin_far[p : p + 1, :] * cos_near[...] + cos_far[p : p + 1, :] * sin_near[...]
+        query = dq[:, p * BLOCK : (p + 1) * BLOCK].T * 0.125
+        pair = jnp.concatenate([query, key_grads[tile][row : row + BLOCK, :]], 1)
+        pair = (pair * cosine - turn_back(pair, lanes) * sine).astype(jnp.bfloat16)
+        value = value_grads[tile][row : row + BLOCK, :]
+        last = jnp.concatenate([value, jnp.zeros_like(value)], 1).astype(jnp.bfloat16)
+        delta[target, 0:128] = pair
+        delta[target, 128:256] = last
+        total[:, 0:128] += jnp.sum(pair.astype(jnp.float32), 0, keepdims=True)
+        total[:, 128:256] += jnp.sum(last.astype(jnp.float32), 0, keepdims=True)
+
+
+def finish(slots, dq, angles, key_grads, value_grads):
+    rows = dq.shape[1]
+    return pl.pallas_call(
+        functools.partial(finish_kernel, len(key_grads)),
+        in_specs=[SMEM] + [VMEM] * (5 + 2 * len(key_grads)),
+        out_specs=[VMEM] * 2,
+        out_shape=[shaped((rows, 256), jnp.bfloat16), shaped((1, 256), jnp.float32)],
+        compiler_params=pltpu.CompilerParams(vmem_limit_bytes=40 * MIB),
+        cost_estimate=pl.CostEstimate(flops=0, bytes_accessed=rows * 2048, transcendentals=0),
+        name="joint_delta",
+    )(slots, dq, *angles, *key_grads, *value_grads)
+
+
+def assemble_kernel(owners, blob, *refs):
+    shrink, dense, expand = refs[-6:-3]
+    wide, tall, sems = refs[-3:]
+    group = owners[2]
+    hidden = expand.shape[1] // 2
+    size = blob.shape[0] // 2
+
+    def dense_copy(n):
+        return pltpu.make_async_copy(
+            wide.at[n, pl.ds(128, 64)],
+            dense.at[pl.ds(pl.multiple_of(lax.rem(owners[n], 8) * 64, 64), 64)],
+            sems.at[n, 3],
+        )
+
+    copies = []
+    for n in range(2):
+        wide[n] = blob[n * size : n * size + 192, :].astype(jnp.float32)
+        for quarter in range(4):
+            tall[n, quarter * 128 : (quarter + 1) * 128, :] = blob[
+                n * size + 192 : n * size + 320, quarter * 256 : (quarter + 1) * 256
+            ].astype(jnp.float32)
+        start = pl.multiple_of(owners[n] * 128, 128)
+        copies += [
+            pltpu.make_async_copy(
+                wide.at[n, pl.ds(0, 128)], shrink.at[pl.ds(start, 128)], sems.at[n, 0]
+            ),
+            pltpu.make_async_copy(
+                tall.at[n, :, pl.ds(0, 128)], expand.at[:, pl.ds(start, 128)], sems.at[n, 1]
+            ),
+            pltpu.make_async_copy(
+                tall.at[n, :, pl.ds(128, 128)],
+                expand.at[:, pl.ds(pl.multiple_of(hidden + start, 128), 128)],
+                sems.at[n, 2],
+            ),
+        ]
+        for copy in copies[-3:]:
+            copy.start()
+
+        @pl.when(owners[n] // 8 == group)
+        def _(n=n):
+            dense_copy(n).start()
+
+    for copy in copies:
+        copy.wait()
+    for n in range(2):
+
+        @pl.when(owners[n] // 8 == group)
+        def _(n=n):
+            dense_copy(n).wait()
+
+
+def assemble(owners, blob, shapes, outs):
+    return pl.pallas_call(
+        assemble_kernel,
+        in_specs=[SMEM, VMEM] + [ANY] * (0 if outs is None else 3),
+        out_specs=[ANY] * 3,
+        out_shape=[shaped(s, jnp.float32) for s in shapes],
+        scratch_shapes=[
+            pltpu.VMEM((2, 192, 1024), jnp.float32),
+            pltpu.VMEM((2, 512, 256), jnp.float32),
+            pltpu.SemaphoreType.DMA((2, 4)),
+        ],
+        input_output_aliases={} if outs is None else {2 + i: i for i in range(3)},
+        compiler_params=pltpu.CompilerParams(vmem_limit_bytes=40 * MIB),
+        cost_estimate=pl.CostEstimate(flops=0, bytes_accessed=640 * 6144, transcendentals=0),
+        name="place_gradients",
+    )(owners, blob, *(outs or ()))
+
+
+def assemble_joint_kernel(count, owners, *refs):
+    blobs = refs[:count]
+    joint, buffer, sems = refs[count:]
+    width = joint.shape[1] // 3
+    size = blobs[0].shape[0] // 2
+    copies = []
+    for n in range(2 * count):
+        owner = owners[n]
+        first = (n % 2) * size
+        buffer[n] = blobs[n // 2][first : first + 256, :].astype(jnp.float32)
+        top = pl.multiple_of(lax.rem(owner, 2) * 256, 256)
+        for part in range(3):
+            start = pl.multiple_of(part * width + (owner // 2) * 128, 128)
+            copies.append(
+                pltpu.make_async_copy(
+                    buffer.at[n, :, pl.ds(part * 128, 128)],
+                    joint.at[pl.ds(top, 256), pl.ds(start, 128)],
+                    sems.at[n, part],
+                )
+            )
+            copies[-1].start()
+    for copy in copies:
+        copy.wait()
+
+
+def assemble_joint(owners, blobs, shape):
+    count = len(blobs)
+    return pl.pallas_call(
+        functools.partial(assemble_joint_kernel, count),
+        in_specs=[SMEM] + [VMEM] * count,
+        out_specs=ANY,
+        out_shape=shaped(shape, jnp.float32),
+        scratch_shapes=[
+            pltpu.VMEM((2 * count, 256, 384), jnp.float32),
+            pltpu.SemaphoreType.DMA((2 * count, 3)),
+        ],
+        compiler_params=pltpu.CompilerParams(vmem_limit_bytes=40 * MIB),
+        cost_estimate=pl.CostEstimate(
+            flops=0, bytes_accessed=count * 512 * 384 * 6, transcendentals=0
+        ),
+        name="place_joint_gradient",
+    )(owners, *blobs)
+
+
+def split_heads(
+    tokens,
+    cotangent,
+    first_gain,
+    first_shift,
+    second_gain,
+    second_shift,
+    joint_weight,
+    joint_bias,
+    dense_weight,
+    dense_bias,
+    expand_weight,
+    expand_bias,
+    shrink_weight,
+    shrink_bias,
+    block_order,
+):
+    f32, bf16 = jnp.float32, jnp.bfloat16
+    me = lax.axis_index("ctx")
+    group = lax.axis_index("fsdp")
+    core = me % 2
+    rows, width = tokens.shape[1:]
+    total_rows = rows * 16
+    hidden = expand_weight.shape[1] // 2
+    own_tokens, own_upstream = tokens[0], cotangent[0]
+
+    token_blocks, token_hops = ring_gather(own_tokens, core)
+    upstream_blocks, upstream_hops = ring_gather(
+        own_upstream, core, (token_hops[2], token_hops[3], None, None)
+    )
+
+    owners = piece_owners(me)
+    blocks = block_order.reshape(16, 2)[owners].reshape(32)
+    slots = jnp.sum(
+        jnp.where(
+            blocks[None, :] == jnp.arange(32, dtype=jnp.int32)[:, None],
+            jnp.arange(32, dtype=jnp.int32)[None, :],
+            0,
+        ),
+        1,
+    )
+
+    def both(mine, received, axis):
+        return jnp.concatenate(
+            [jnp.where(group == 0, mine, received), jnp.where(group == 0, received, mine)], axis
+        )
+
+    heads = [cut(joint_weight, i * width + (me // 2) * 128, 128, 1) for i in range(3)]
+    tall = jnp.concatenate(
+        [jnp.where(core == 0, h[:, :64], h[:, 64:]) for h in heads]
+        + [jnp.zeros((width // 2, 64), bf16)]
+        + [cut(expand_weight, i * hidden + me * 128, 128, 1) for i in range(2)],
+        1,
+    )
+    vector = jnp.concatenate(
+        [
+            first_gain,
+            first_shift,
+            second_gain,
+            second_shift,
+            dense_bias,
+            shrink_bias,
+            joint_bias,
+            expand_bias,
+            jnp.zeros((16 * 1024 - 13 * 512,), bf16),
+        ]
+    ).reshape(16, 1024)
+    flat = jnp.concatenate(
+        [cut(shrink_weight, me * 128, 128, 0), cut(dense_weight, (me % 8) * 64, 64, 0), vector], 0
+    )
+    tall_other, flat_other = other(tall), other(flat)
+    tall = both(tall, tall_other, 0)
+    joint_c, expand_c = tall[:, :256], tall[:, 256:]
+    shrink_c = both(flat[:128], flat_other[:128], 0)
+    dense_c = jnp.where(group == me // 8, flat[128:192], flat_other[128:192])
+    vectors = both(
+        vector.reshape(-1, 512)[None, :13], flat_other[192:].reshape(-1, 512)[None, :13], 0
+    ).astype(f32)
+    gain_one, shift_one, gain_two, shift_two, dense_shift, shrink_shift = (
+        vectors[:, i, :].reshape(-1) for i in range(6)
+    )
+    joint_b = jnp.pad(
+        cut(vectors[:, 6:9, :].reshape(3, 16, 64), me, 1, 1).reshape(1, 192), ((0, 0), (0, 64))
+    )
+    expand_b = cut(vectors[:, 9:13, :].reshape(2, 16, 128), me, 1, 1).reshape(1, 256)
+    norms = jnp.concatenate(
+        [jnp.stack([gain_one, shift_one, gain_two, shift_two]), jnp.zeros((4, width), f32)], 0
+    )
+
+    outs = None
+    for index, block in enumerate(token_blocks):
+        outs = pre(index, block, norms, joint_c, joint_b, expand_c, expand_b, outs, 8)
+    normed_one, normed_two, joint, activated, slope = outs
+
+    angles = tables(jnp.arange(total_rows // BLOCK) * BLOCK) + tables(jnp.arange(BLOCK))
+    query, key, value = turn(blocks, joint, angles)
+    mixed, outs, sums = None, [], []
+    for index in range(4):
+        gate = upstream_hops[index - 1] if index else None
+        mixed, out, lse = attention_forward(index, slots, query, key, value, mixed, gate)
+        outs.append(out)
+        sums.append(lse)
+    lse = jnp.concatenate(
+        [s[:, :TILE] for s in sums] + [s[:, TILE:] for s in sums[::-1]], 1
+    )
+
+    branch = jnp.concatenate([activated, mixed], 1)
+    back = jnp.concatenate([shrink_c, dense_c], 0)
+    out_sum, out_hops = ring_scatter(branch, back, core, (upstream_hops[3], None, None, None))
+    output = own_tokens.astype(f32) + out_sum + dense_shift + shrink_shift
+
+    expand_delta, mixed_grad, shrink_grad, dense_grad, column_sum, expand_sum = post(
+        upstream_blocks, slope, activated, mixed, shrink_c, dense_c
+    )
+    expand_grad = tn(normed_two, expand_delta)
+
+    def half_of(values, which, axis):
+        size = values.shape[axis] // 2
+        return cut(values, which * size, size, axis)
+
+    def sum_halves(values, axis):
+        sent = half_of(values, 1 - group, axis).astype(bf16)
+        return half_of(values, group, axis) + other(sent).astype(f32)
+
+    shrink_half = sum_halves(shrink_grad, 0).astype(bf16)
+    dense_half = (dense_grad + other(dense_grad.astype(bf16)).astype(f32)).astype(bf16)
+    expand_half = sum_halves(expand_grad, 0).astype(bf16)
+    blob = jnp.concatenate(
+        [
+            shrink_half,
+            dense_half,
+            jnp.concatenate([expand_half[i * 128 : (i + 1) * 128] for i in range(4)], 1),
+        ],
+        0,
+    )
+    blob_blocks, blob_hops = ring_gather(blob, core, (out_hops[2], out_hops[3], None, None))
+    placed = None
+    shapes = ((hidden, width), (width // 2, width), (width // 2, 2 * hidden))
+    for index, block in enumerate(blob_blocks):
+        some = jnp.concatenate([owners[2 * index : 2 * index + 2], group[None]]).astype(jnp.int32)
+        placed = assemble(some, block, shapes, placed)
+    shrink_total, dense_total, expand_total = placed
+
+    out_grad, inner = sort_grad(slots, mixed_grad, outs)
+    dq, key_grads, value_grads = None, [], []
+    for index in range(4):
+        gate = out_hops[index - 1] if index else None
+        dq, dk, dv = attention_backward(
+            index, query, key, value, out_grad, inner, lse, dq, gate
+        )
+        key_grads.append(dk)
+        value_grads.append(dv)
+    joint_delta, joint_sum = finish(slots, dq, angles, key_grads, value_grads)
+    joint_grad = tn(normed_one, joint_delta)
+
+    delta = jnp.concatenate([joint_delta, expand_delta], 1)
+    scaled = jnp.concatenate(
+        [
+            (joint_c.astype(f32) * gain_one[:, None]).astype(bf16),
+            (expand_c.astype(f32) * gain_two[:, None]).astype(bf16),
+        ],
+        1,
+    ).T
+    in_sum, in_hops = ring_scatter(delta, scaled, core, (blob_hops[2], blob_hops[3], None, None))
+    mine = own_tokens.astype(f32)
+    mine = mine - jnp.mean(mine, -1, keepdims=True)
+    scale = lax.rsqrt(jnp.mean(mine * mine, -1, keepdims=True) + epsilon)
+    mine = mine * scale
+    term = scale * (
+        in_sum
+        - jnp.mean(in_sum, -1, keepdims=True)
+        - mine * jnp.mean(in_sum * mine, -1, keepdims=True)
+    )
+    tokens_grad = (own_upstream.astype(f32) + term).astype(bf16)
+
+    def norm_grads(weight, grad, total, gain, shift):
+        weight = weight.astype(f32)
+        shift_grad = jnp.sum(weight * total, 1)
+        return (jnp.sum(weight * grad, 1) - shift * shift_grad) / gain, shift_grad
+
+    gain_one_grad, shift_one_grad = norm_grads(joint_c, joint_grad, joint_sum, gain_one, shift_one)
+    gain_two_grad, shift_two_grad = norm_grads(
+        expand_c, expand_grad, expand_sum, gain_two, shift_two
+    )
+    norm_part = jnp.stack([gain_one_grad, shift_one_grad, gain_two_grad, shift_two_grad]).reshape(
+        4, 2, width // 2
+    )
+    column_part = column_sum.reshape(2, width // 2)
+    bias_part = jnp.concatenate([joint_sum[0, :192], expand_sum[0]])
+
+    def pack(which):
+        return jnp.concatenate(
+            [
+                cut(norm_part, which, 1, 1).reshape(-1),
+                cut(column_part, which, 1, 0).reshape(-1),
+                bias_part,
+                jnp.zeros((32 * 384 - 5 * (width // 2) - 448,), f32),
+            ]
+        ).reshape(32, 384)
+
+    packed = pack(group) + other(pack(1 - group).astype(bf16)).astype(f32)
+
+    joint_half = sum_halves(joint_grad, 0)[:, :192].astype(bf16)
+    kept = half_of(joint_half, core, 0)
+    received = swap(half_of(joint_half, 1 - core, 0))
+    low = jnp.where(core == 0, kept, received).reshape(-1, 3, 1, 64)
+    high = jnp.where(core == 0, received, kept).reshape(-1, 3, 1, 64)
+    joint_blob = jnp.concatenate([low, high], 2).reshape(-1, 384)
+    joint_blob = jnp.concatenate([joint_blob, packed.astype(bf16)], 0)
+    joint_blocks, _ = ring_gather(joint_blob, core)
+    joint_total = assemble_joint(owners, joint_blocks, (width // 2, 3 * width))
+
+    parts = jnp.concatenate(
+        [
+            jnp.stack([b[256:288], b[544:576]]).reshape(2, -1).astype(f32)
+            for b in joint_blocks
+        ],
+        0,
+    )
+    small = width // 2
+    totals = jnp.sum(parts[:, : 4 * small], 0)
+    order = jnp.zeros((16, 16), f32).at[owners, jnp.arange(16)].set(1.0)
+    biases = jnp.sum(order[:, :, None] * parts[None, :, 5 * small : 5 * small + 448], 1)
+    joint_bias_total = jnp.transpose(biases[:, :192].reshape(16, 3, 64), (1, 0, 2)).reshape(-1)
+    expand_bias_total = jnp.transpose(biases[:, 192:].reshape(16, 2, 128), (1, 0, 2)).reshape(-1)
+    column_total = packed.reshape(-1)[4 * small : 5 * small]
+
+    return (
+        output.astype(bf16)[None],
+        tokens_grad[None],
+        totals[:small],
+        totals[small : 2 * small],
+        totals[2 * small : 3 * small],
+        totals[3 * small :],
+        joint_total,
+        half_of(joint_bias_total, group, 0),
+        dense_total,
+        column_total,
+        expand_total,
+        half_of(expand_bias_total, group, 0),
+        shrink_total,
+        column_total,
+    )
+
 
 def solution(mesh):
+    fits = mesh.shape["ctx"] == HEADS and mesh.shape["fsdp"] == 2
     return jax.shard_map(
-        shards,
+        split_heads if fits else shards,
         mesh=mesh,
         in_specs=(
             P("fsdp", "ctx", None),

time: 1410 us -> 447 us (0.32)
  waiting for transfers between devices: 824 us -> 88.6 us
  matrix products: 329 us -> 47.7 us
  Pallas kernels: 0 us -> 128 us
  blocking collectives: 105 us -> 0 us
  starting transfers between devices: 0.7 us -> 54.5 us
  local copies, waits for them, and re-layouts: 45.4 us -> 71.6 us
  loops' own time: 21.9 us -> 0 us
  other arithmetic: 58.5 us -> 42.8 us
    reduce_scatter x6 -> x0, waiting for transfers between devices: 459 us -> none  [the longest x1 105 us: shards(): lax.psum_scatter(value_grads.astype(jnp.bfloat16), 'ctx', scatter_dimensi...]
    dot_general x124 -> x20, matrix products: 329 us -> 47.7 us  [the longest x18 37.7 us: nn(): return jnp.dot(left_side, right_side, preferred_element_type=jnp.float32)]
    all_gather x6 -> x0, waiting for transfers between devices: 229 us -> none  [the longest x1 78.3 us: shards(): lax.all_gather(key_rows, 'ctx', axis=0, tiled=True)]
    psum x1 -> x0, waiting for transfers between devices: 133 us -> none  [shards(): lax.psum(joint_part.astype(jnp.bfloat16), 'ctx').astype(jnp.float32)]
    pallas_call x0 -> x29, Pallas kernels: none -> 128 us  [the longest x4 29.8 us: attention_backward(): pl.pallas_call(functools.partial(backward_kernel, index, dq is None), in_...]
    ppermute x0 -> x62, waiting for transfers between devices: none -> 88.6 us  [the longest x24 80 us: hop(): return lax.ppermute(values, 'ctx', RING)]
    psum x1 -> x0, blocking collectives: 61.9 us -> none  [shards(): lax.psum(gain_one_part.astype(jnp.bfloat16), 'ctx').astype(jnp.float32)]
    ppermute x0 -> x62, starting transfers between devices: none -> 54.5 us  [the longest x24 39.8 us: hop(): return lax.ppermute(values, 'ctx', RING)]
  transfers between devices with their start and end apart: 13 -> 62, of which waited for: 11 -> 16; matrix products, arithmetic and copies ran while one was open for 29% -> 33% of each run, Pallas kernels for 0% -> 29%
where the time goes in v2:
time: 447 us; the launch traced here: 438 us
  Pallas kernels  128 us (29%)
  waiting for transfers between devices  88.6 us (20%)
  local copies, waits for them, and re-layouts  71.6 us (16%)
  starting transfers between devices  54.5 us (12%)
  matrix products  47.7 us (11%)
  other arithmetic  42.8 us (10%)
    ppermute x24, waiting for transfers between devices, hop(): return lax.ppermute(values, 'ctx', RING)  80 us
    ppermute x24, starting transfers between devices, hop(): return lax.ppermute(values, 'ctx', RING)  39.8 us
    dot_general x18, matrix products, nn(): return jnp.dot(left_side, right_side, preferred_element_type=jnp.float32)  37.7 us
    unnamed x261, local copies, waits for them, and re-layouts  36.9 us
    pallas_call x4, Pallas kernels, attention_backward(): pl.pallas_call(functools.partial(backward_kernel, index, dq is None), in_...  29.8 us
    pallas_call x4, Pallas kernels, attention_forward(): pl.pallas_call(functools.partial(forward_kernel, index), in_specs=[SMEM]...  28.1 us
    pallas_call x8, Pallas kernels, pre(): pl.pallas_call(pre_kernel, grid=(2,), in_specs=[pl.BlockSpec((step, width...  23 us
    pallas_call x8, Pallas kernels, assemble(): pl.pallas_call(assemble_kernel, in_specs=[SMEM, VMEM] + [ANY] * (0 if out...  19.7 us
  transfers between devices with their start and end apart: 62, of which 16 were waited for; matrix products, arithmetic and copies ran while one was open for 33% of the time, Pallas kernels for 29%

profile of v2, /device:TPU:0, one launch (start us, length us, event | category | flops | bytes accessed | tf_op | source)
XLA Modules:
  0.0 437.9 jit_solution(3704232209108468132)
XLA Ops:
  11.2 2.6 collective-permute-start.6
  29.4 8.0 %collective-permute-done.1.x = bf16[512,1024]{1,0:T(8,128)(2,1)S(1)} collective-permute-done((bf16[512,1024]{1,0:T(8,128)(2,1)S(1)}, bf16[512,1024]{1,0:T(8,128)(2,1)S(1)}, u32[]{:S(2)}, u32[]{:S(2)}) %collective-permute-start.1) | collective-permute-done | bytes 1048608 | tf_op jit(solution)/shard_map/ppermute | solution.py:306
  44.3 7.9 %collective-permute-done.2.x = bf16[512,1024]{1,0:T(8,128)(2,1)S(1)} collective-permute-done((bf16[512,1024]{1,0:T(8,128)(2,1)S(1)}, bf16[512,1024]{1,0:T(8,128)(2,1)S(1)}, u32[]{:S(2)}, u32[]{:S(2)}) %collective-permute-start.2) | collective-permute-done | bytes 1048608 | tf_op jit(solution)/shard_map/ppermute | solution.py:306
  59.1 8.0 %collective-permute-done.3.x = bf16[512,1024]{1,0:T(8,128)(2,1)} collective-permute-done((bf16[512,1024]{1,0:T(8,128)(2,1)S(1)}, bf16[512,1024]{1,0:T(8,128)(2,1)}, u32[]{:S(2)}, u32[]{:S(2)}) %collective-permute-start.3) | collective-permute-done | bytes 1048608 | tf_op jit(solution)/shard_map/ppermute | solution.py:306
  70.1 3.0 maximum_select_fusion.2.refs_0_
  83.5 3.4 norms_joint_hidden.10
  89.3 3.4 norms_joint_hidden.12
  92.7 3.4 norms_joint_hidden.13
  99.1 3.4 norms_joint_hidden.14
  104.9 6.1 %rotary_and_sort.1 = (bf16[4096,64]{1,0:T(8,128)(2,1)S(1)}, bf16[4096,64]{1,0:T(8,128)(2,1)S(1)}, bf16[4096,64]{1,0:T(8,128)(2,1)S(1)}) custom-call(s32[32]{0:T(128)S(1)} %eq.28.blocks, f32[4096,256]{1,0:T(8,128)S(1)} %get-tuple-element.158.joint, f32[32,128]{1,0:T(8,128)S(1)} %get-tuple-element.299.cos_far, f32[32,128]{1,0:T(8,128)S(1)} %get-tuple-element.298.sin_far, ...), custom_call_target="tpu_custom_call" | custom-call | bytes 8388608 | tf_op jit(solution)/shard_map/rotary_and_sort/pallas_call | solution.py:502
  111.0 7.1 %attention_forward.4 = (bf16[4096,64]{1,0:T(8,128)(2,1)S(1)}, f32[64,1024]{1,0:T(8,128)S(1)}, f32[1,1024]{1,0:T(1,128)S(1)}) custom-call(s32[32]{0:T(128)S(1)} %select_reduce_fusion.slots, bf16[4096,64]{1,0:T(8,128)(2,1)S(1)} %get-tuple-element.159.q, bf16[4096,64]{1,0:T(8,128)(2,1)S(1)} %get-tuple-element.160.k, bf16[4096,64]{1,0:T(8,128)(2,1)S(1)} %get-tuple-element.161.v), custom_call_target="tpu_custom_call" | custom-call | flops 4294967296 | bytes 4194304 | tf_op jit(solution)/shard_map/attention_forward/pallas_call | solution.py:570
  118.3 6.9 %attention_forward.5 = (bf16[4096,64]{1,0:T(8,128)(2,1)S(1)}, f32[64,1024]{1,0:T(8,128)S(1)}, f32[1,1024]{1,0:T(1,128)S(1)}) custom-call(s32[32]{0:T(128)S(1)} %select_reduce_fusion.slots, bf16[4096,64]{1,0:T(8,128)(2,1)S(1)} %get-tuple-element.159.q, bf16[4096,64]{1,0:T(8,128)(2,1)S(1)} %get-tuple-element.160.k, ...), custom_call_target="tpu_custom_call", output_to_operand_aliasing={{0}: (4, {})} | custom-call | flops 4294967296 | bytes 4194304 | tf_op jit(solution)/shard_map/attention_forward/pallas_call | solution.py:570
  127.2 7.1 %attention_forward.6 = (bf16[4096,64]{1,0:T(8,128)(2,1)S(1)}, f32[64,1024]{1,0:T(8,128)S(1)}, f32[1,1024]{1,0:T(1,128)S(1)}) custom-call(s32[32]{0:T(128)S(1)} %select_reduce_fusion.slots, bf16[4096,64]{1,0:T(8,128)(2,1)S(1)} %get-tuple-element.159.q, bf16[4096,64]{1,0:T(8,128)(2,1)S(1)} %get-tuple-element.160.k, ...), custom_call_target="tpu_custom_call", output_to_operand_aliasing={{0}: (4, {})} | custom-call | flops 4294967296 | bytes 4194304 | tf_op jit(solution)/shard_map/attention_forward/pallas_call | solution.py:570
  134.3 6.0 %collective-permute-done.14.refs_1_.refs_5_ = bf16[512,1024]{1,0:T(8,128)(2,1)S(1)} collective-permute-done((bf16[512,1024]{1,0:T(8,128)(2,1)S(1)}, bf16[512,1024]{1,0:T(8,128)(2,1)S(1)}, u32[]{:S(2)}, u32[]{:S(2)}) %collective-permute-start.14) | collective-permute-done | bytes 1048608 | tf_op jit(solution)/shard_map/ppermute | solution.py:306
  141.9 7.1 %attention_forward.7 = (bf16[4096,64]{1,0:T(8,128)(2,1)S(1)}, f32[64,1024]{1,0:T(8,128)S(1)}, f32[1,1024]{1,0:T(1,128)S(1)}) custom-call(s32[32]{0:T(128)S(1)} %select_reduce_fusion.slots, bf16[4096,64]{1,0:T(8,128)(2,1)S(1)} %get-tuple-element.159.q, bf16[4096,64]{1,0:T(8,128)(2,1)S(1)} %get-tuple-element.160.k, ...), custom_call_target="tpu_custom_call", output_to_operand_aliasing={{0}: (4, {})} | custom-call | flops 4294967296 | bytes 4194304 | tf_op jit(solution)/shard_map/attention_forward/pallas_call | solution.py:570
  159.7 4.9 %collective-permute-done.20.refs_1_ = bf16[256,1024]{1,0:T(8,128)(2,1)S(1)} collective-permute-done((bf16[256,1024]{1,0:T(8,128)(2,1)S(1)}, bf16[256,1024]{1,0:T(8,128)(2,1)S(1)}, u32[]{:S(2)}, u32[]{:S(2)}) %collective-permute-start.20) | collective-permute-done | bytes 524320 | tf_op jit(solution)/shard_map/ppermute | solution.py:306
  164.5 2.8 add_convert_fusion.5
  169.3 13.0 %cotangent_products.1 = (bf16[4096,256]{1,0:T(8,128)(2,1)}, bf16[4096,64]{1,0:T(8,128)(2,1)S(1)}, f32[256,1024]{1,0:T(8,128)S(1)}, f32[64,1024]{1,0:T(8,128)S(1)...) custom-call(bf16[512,1024]{1,0:T(8,128)(2,1)} %maximum_select_fusion.2.refs_0_, ...), custom_call_target="tpu_custom_call" | custom-call | flops 5368709120 | bytes 16777216 | tf_op jit(solution)/shard_map/cotangent_products/pallas_call | solution.py:627
  182.2 6.6 %fusion.19 = (f32[1024]{0:T(1024)S(1)}, f32[1024]{0:T(1024)S(1)}, f32[1024,256]{1,0:T(8,128)S(1)}) fusion(bf16[1024,256]{1,0:T(8,128)(2,1)S(1)} %get-tuple-element.243.expand_w, f32[256]{0:T(256)S(1)} %bitcast.163, bf16[4096,1024]{1,0:T(8,128)(2,1)} %get-tuple-element.197, bf16[4096,256]{1,0:T(8,128)(2,1)} %get-tuple-element.194), kind=kOutput, calls=%fused_computation.51 | convolution fusion | flops 2148792320 | bytes 12067840 | tf_op jit(solution)/shard_map/dot_general | solution.py:409
  192.0 7.4 %attention_backward.4 = (f32[64,4096]{1,0:T(8,128)S(1)}, f32[1024,64]{1,0:T(8,128)S(1)}, f32[1024,64]{1,0:T(8,128)S(1)}) custom-call(bf16[4096,64]{1,0:T(8,128)(2,1)S(1)} %get-tuple-element.159.q, bf16[4096,64]{1,0:T(8,128)(2,1)S(1)} %get-tuple-element.160.k, bf16[4096,64]{1,0:T(8,128)(2,1)S(1)} %get-tuple-element.161.v, ...), custom_call_target="tpu_custom_call" | custom-call | flops 10737418240 | bytes 8388608 | tf_op jit(solution)/shard_map/attention_backward/pallas_call | solution.py:730
  201.3 5.1 %collective-permute-done.33 = bf16[128,1024]{1,0:T(8,128)(2,1)S(1)} collective-permute-done((bf16[128,1024]{1,0:T(8,128)(2,1)S(1)}, bf16[128,1024]{1,0:T(8,128)(2,1)S(1)}, u32[]{:S(2)}, u32[]{:S(2)}) %collective-permute-start.33) | collective-permute-done | bytes 262176 | tf_op jit(solution)/shard_map/ppermute | solution.py:314
  207.5 7.3 %attention_backward.5 = (f32[64,4096]{1,0:T(8,128)S(1)}, f32[1024,64]{1,0:T(8,128)S(1)}, f32[1024,64]{1,0:T(8,128)S(1)}) custom-call(bf16[4096,64]{1,0:T(8,128)(2,1)S(1)} %get-tuple-element.159.q, bf16[4096,64]{1,0:T(8,128)(2,1)S(1)} %get-tuple-element.160.k, bf16[4096,64]{1,0:T(8,128)(2,1)S(1)} %get-tuple-element.161.v, ...), custom_call_target="tpu_custom_call" | custom-call | flops 10737418240 | bytes 8388608 | tf_op jit(solution)/shard_map/attention_backward/pallas_call | solution.py:730
  217.8 2.7 add_convert_fusion.4
  222.3 7.5 %maximum_select_fusion.blob = bf16[640,1024]{1,0:T(8,128)(2,1)S(1)} fusion(bf16[320,1024]{1,0:T(8,128)(2,1)} %collective-permute-done.36, bf16[128,256]{1,0:T(8,128)(2,1)S(1)} %copy-done.69, bf16[128,256]{1,0:T(8,128)(2,1)S(1)} %copy-done.71, bf16[128,256]{1,0:T(8,128)(2,1)S(1)} %copy-done.73, bf16[128,256]{1,0:T(8,128)(2,1)S(1)} %copy-done.67, ...), kind=kLoop, calls=%fused_computation.28 | loop fusion | flops 19005440 | bytes 2621441 | tf_op jit(solution)/shard_map/jit(_where)/select_n | solution.py:328
  231.1 7.5 %attention_backward.6 = (f32[64,4096]{1,0:T(8,128)S(1)}, f32[1024,64]{1,0:T(8,128)S(1)}, f32[1024,64]{1,0:T(8,128)S(1)}) custom-call(bf16[4096,64]{1,0:T(8,128)(2,1)S(1)} %copy-done.26, bf16[4096,64]{1,0:T(8,128)(2,1)S(1)} %copy-done.28, bf16[4096,64]{1,0:T(8,128)(2,1)S(1)} %copy-done.30, bf16[4096,64]{1,0:T(8,128)(2,1)S(1)} %copy-done.32, ...), custom_call_target="tpu_custom_call" | custom-call | flops 10737418240 | bytes 8388608 | tf_op jit(solution)/shard_map/attention_backward/pallas_call | solution.py:730
  240.5 3.2 add_convert_fusion.3
  245.4 7.5 %attention_backward.7 = (f32[64,4096]{1,0:T(8,128)S(1)}, f32[1024,64]{1,0:T(8,128)S(1)}, f32[1024,64]{1,0:T(8,128)S(1)}) custom-call(bf16[4096,64]{1,0:T(8,128)(2,1)S(1)} %copy-done.26, bf16[4096,64]{1,0:T(8,128)(2,1)S(1)} %copy-done.28, bf16[4096,64]{1,0:T(8,128)(2,1)S(1)} %copy-done.30, bf16[4096,64]{1,0:T(8,128)(2,1)S(1)} %copy-done.32, ...), custom_call_target="tpu_custom_call" | custom-call | flops 10737418240 | bytes 8388608 | tf_op jit(solution)/shard_map/attention_backward/pallas_call | solution.py:730
  252.9 4.2 joint_delta.1
  258.5 3.3 fusion.63
  275.6 10.2 %collective-permute-done.38.blob = bf16[640,1024]{1,0:T(8,128)(2,1)} collective-permute-done((bf16[640,1024]{1,0:T(8,128)(2,1)}, bf16[640,1024]{1,0:T(8,128)(2,1)}, u32[]{:S(2)}, u32[]{:S(2)}) %collective-permute-start.38) | collective-permute-done | bytes 1310752 | tf_op jit(solution)/shard_map/ppermute | solution.py:306
  293.3 2.8 collective-permute-done.46
  297.3 2.5 fusion
  299.9 4.0 collective-permute-done.39.blob
  313.3 3.6 add_convert_fusion.2
  317.0 3.4 collective-permute-done.41
  325.8 2.8 convolution_convert_fusion.5
  330.4 9.7 %collective-permute-done.50.refs_1_ = bf16[576,384]{1,0:T(8,128)(2,1)S(1)} collective-permute-done((bf16[576,384]{1,0:T(8,128)(2,1)S(1)}, bf16[576,384]{1,0:T(8,128)(2,1)S(1)}, u32[]{:S(2)}, u32[]{:S(2)}) %collective-permute-start.50) | collective-permute-done | bytes 442400 | tf_op jit(solution)/shard_map/ppermute | solution.py:306
  343.1 2.7 add_convert_fusion.1
  350.3 3.0 place_gradients.9
  357.6 3.5 collective-permute-done.43
  361.1 3.2 add_convert_fusion
  370.4 11.4 %collective-permute-done.56 = bf16[288,384]{1,0:T(8,128)(2,1)S(1)} collective-permute-done((bf16[288,384]{1,0:T(8,128)(2,1)S(1)}, bf16[288,384]{1,0:T(8,128)(2,1)S(1)}, u32[]{:S(2)}, u32[]{:S(2)}) %collective-permute-start.56) | collective-permute-done | bytes 221216 | tf_op jit(solution)/shard_map/ppermute | solution.py:306
  386.4 4.2 concatenate.226
  410.9 3.6 place_joint_gradient.1
  418.4 2.9 place_gradients.11
  421.3 2.8 place_gradients.12
  426.1 2.8 place_gradients.14
  434.1 2.7 fusion.23
  (528 shorter events, 185.4 us)
Async XLA Ops:
  0.6 21.4 %collective-permute-start = (bf16[256,1024]{1,0:T(8,128)(2,1)}, bf16[256,1024]{1,0:T(8,128)(2,1)S(1)}, u32[]{:S(2)}, u32[]{:S(2)}) collective-permute-start(bf16[256,1024]{1,0:T(8,128)(2,1)} %bitcast.171), channel_id=1, source_target_pairs={{0,2},{2,0},{4,6},{6,4},{8,10},{10,8},{12,14},{14,12},{16,18},{18,... | collective-permute-start | bytes 1572872 | tf_op jit(solution)/shard_map/ppermute | solution.py:310
  11.2 31.7 %collective-permute-start.6 = (bf16[208,1024]{1,0:T(8,128)(2,1)}, bf16[208,1024]{1,0:T(8,128)(2,1)}, u32[]{:S(2)}, u32[]{:S(2)}) collective-permute-start(bf16[208,1024]{1,0:T(8,128)(2,1)} %pad_maximum_fusion.8), channel_id=1, source_target_pairs={{0,1},{1,0},{2,3},{3,2},{4,5},{5,4},{6,7},{7,6},{8,9},{9,8},{10,11... | collective-permute-start | bytes 1277960 | tf_op jit(solution)/shard_map/ppermute | solution.py:314
  17.5 57.3 %collective-permute-start.7 = (bf16[512,512]{1,0:T(8,128)(2,1)}, bf16[512,512]{1,0:T(8,128)(2,1)}, u32[]{:S(2)}, u32[]{:S(2)}) collective-permute-start(bf16[512,512]{1,0:T(8,128)(2,1)} %concatenate.197), channel_id=1, source_target_pairs={{0,1},{1,0},{2,3},{3,2},{4,5},{5,4},{6,7},{7,6},{8,9},{9,8},{10,11... | collective-permute-start | bytes 1572872 | tf_op jit(solution)/shard_map/ppermute | solution.py:314
  17.6 52.5 %collective-permute-start.11 = (bf16[256,1024]{1,0:T(8,128)(2,1)}, bf16[256,1024]{1,0:T(8,128)(2,1)}, u32[]{:S(2)}, u32[]{:S(2)}) collective-permute-start(bf16[256,1024]{1,0:T(8,128)(2,1)} %bitcast.13), channel_id=1, source_target_pairs={{0,2},{2,0},{4,6},{6,4},{8,10},{10,8},{12,14},{14,12},{16,18},{18,... | collective-permute-start | bytes 1572872 | tf_op jit(solution)/shard_map/ppermute | solution.py:310
  22.5 14.9 %collective-permute-start.1 = (bf16[512,1024]{1,0:T(8,128)(2,1)S(1)}, bf16[512,1024]{1,0:T(8,128)(2,1)S(1)}, u32[]{:S(2)}, u32[]{:S(2)}) collective-permute-start(bf16[512,1024]{1,0:T(8,128)(2,1)S(1)} %maximum_select_fusion.1.x), channel_id=1, source_target_pairs={{0,8},{8,16},{16,24},{24,28},{28,20},{20,12},{12,4},{4,0},{2,6},{1... | collective-permute-start | bytes 3145736 | tf_op jit(solution)/shard_map/ppermute | solution.py:306
  37.4 14.8 %collective-permute-start.2 = (bf16[512,1024]{1,0:T(8,128)(2,1)S(1)}, bf16[512,1024]{1,0:T(8,128)(2,1)S(1)}, u32[]{:S(2)}, u32[]{:S(2)}) collective-permute-start(bf16[512,1024]{1,0:T(8,128)(2,1)S(1)} %collective-permute-done.1.x), channel_id=1, source_target_pairs={{0,8},{8,16},{16,24},{24,28},{28,20},{20,12},{12,4},{4,0},{2,6},{1... | collective-permute-start | bytes 3145736 | tf_op jit(solution)/shard_map/ppermute | solution.py:306
  52.2 14.9 %collective-permute-start.3 = (bf16[512,1024]{1,0:T(8,128)(2,1)S(1)}, bf16[512,1024]{1,0:T(8,128)(2,1)}, u32[]{:S(2)}, u32[]{:S(2)}) collective-permute-start(bf16[512,1024]{1,0:T(8,128)(2,1)S(1)} %collective-permute-done.2.x), channel_id=1, source_target_pairs={{0,8},{8,16},{16,24},{24,28},{28,20},{20,12},{12,4},{4,0},{2,6},{1... | collective-permute-start | bytes 3145736 | tf_op jit(solution)/shard_map/ppermute | solution.py:306
  57.9 25.6 %collective-permute-start.10 = (bf16[512,1024]{1,0:T(8,128)(2,1)S(1)}, bf16[512,1024]{1,0:T(8,128)(2,1)}, u32[]{:S(2)}, u32[]{:S(2)}) collective-permute-start(bf16[512,1024]{1,0:T(8,128)(2,1)S(1)} %collective-permute-done.1.x), channel_id=1, source_target_pairs={{0,2},{2,0},{4,6},{6,4},{8,10},{10,8},{12,14},{14,12},{16,18},{18,... | collective-permute-start | bytes 3145736 | tf_op jit(solution)/shard_map/ppermute | solution.py:310
  58.5 30.7 %collective-permute-start.9 = (bf16[512,1024]{1,0:T(8,128)(2,1)S(1)}, bf16[512,1024]{1,0:T(8,128)(2,1)}, u32[]{:S(2)}, u32[]{:S(2)}) collective-permute-start(bf16[512,1024]{1,0:T(8,128)(2,1)S(1)} %collective-permute-done.2.x), channel_id=1, source_target_pairs={{0,2},{2,0},{4,6},{6,4},{8,10},{10,8},{12,14},{14,12},{16,18},{18,... | collective-permute-start | bytes 3145736 | tf_op jit(solution)/shard_map/ppermute | solution.py:310
  73.1 24.1 %collective-permute-start.12 = (bf16[512,1024]{1,0:T(8,128)(2,1)}, bf16[512,1024]{1,0:T(8,128)(2,1)}, u32[]{:S(2)}, u32[]{:S(2)}) collective-permute-start(bf16[512,1024]{1,0:T(8,128)(2,1)} %maximum_select_fusion.2.refs_0_), channel_id=1, source_target_pairs={{0,8},{8,16},{16,24},{24,28},{28,20},{20,12},{12,4},{4,0},{2,6},{1... | collective-permute-start | bytes 3145736 | tf_op jit(solution)/shard_map/ppermute | solution.py:306
  74.8 24.3 %collective-permute-start.8 = (bf16[512,1024]{1,0:T(8,128)(2,1)}, bf16[512,1024]{1,0:T(8,128)(2,1)}, u32[]{:S(2)}, u32[]{:S(2)}) collective-permute-start(bf16[512,1024]{1,0:T(8,128)(2,1)} %collective-permute-done.3.x), channel_id=1, source_target_pairs={{0,2},{2,0},{4,6},{6,4},{8,10},{10,8},{12,14},{14,12},{16,18},{18,... | collective-permute-start | bytes 3145736 | tf_op jit(solution)/shard_map/ppermute | solution.py:310
  77.5 18.6 %collective-permute-start.5 = (bf16[256,1024]{1,0:T(8,128)(2,1)}, bf16[256,1024]{1,0:T(8,128)(2,1)S(1)}, u32[]{:S(2)}, u32[]{:S(2)}) collective-permute-start(bf16[256,1024]{1,0:T(8,128)(2,1)} %collective-permute-done.4), channel_id=1, source_target_pairs={{0,2},{2,0},{4,6},{6,4},{8,10},{10,8},{12,14},{14,12},{16,18},{18,... | collective-permute-start | bytes 1572872 | tf_op jit(solution)/shard_map/ppermute | solution.py:310
  97.2 28.0 %collective-permute-start.13 = (bf16[512,1024]{1,0:T(8,128)(2,1)}, bf16[512,1024]{1,0:T(8,128)(2,1)S(1)}, u32[]{:S(2)}, u32[]{:S(2)}) collective-permute-start(bf16[512,1024]{1,0:T(8,128)(2,1)} %collective-permute-done.12.refs_1_), channel_id=1, source_target_pairs={{0,8},{8,16},{16,24},{24,28},{28,20},{20,12},{12,4},{4,0},{2,6},{1... | collective-permute-start | bytes 3145736 | tf_op jit(solution)/shard_map/ppermute | solution.py:306
  118.1 49.2 %collective-permute-start.25 = (bf16[512,1024]{1,0:T(8,128)(2,1)}, bf16[512,1024]{1,0:T(8,128)(2,1)S(1)}, u32[]{:S(2)}, u32[]{:S(2)}) collective-permute-start(bf16[512,1024]{1,0:T(8,128)(2,1)} %collective-permute-done.12.refs_1_), channel_id=1, source_target_pairs={{0,2},{2,0},{4,6},{6,4},{8,10},{10,8},{12,14},{14,12},{16,18},{18,... | collective-permute-start | bytes 3145736 | tf_op jit(solution)/shard_map/ppermute | solution.py:310
  125.2 15.1 %collective-permute-start.14 = (bf16[512,1024]{1,0:T(8,128)(2,1)S(1)}, bf16[512,1024]{1,0:T(8,128)(2,1)S(1)}, u32[]{:S(2)}, u32[]{:S(2)}) collective-permute-start(bf16[512,1024]{1,0:T(8,128)(2,1)S(1)} %collective-permute-done.13.refs_1_.refs_3_), channel_id=1, source_target_pairs={{0,8},{8,16},{16,24},{24,28},{28,20},{20,12},{12,4},{4,0},{2,6},{1... | collective-permute-start | bytes 3145736 | tf_op jit(solution)/shard_map/ppermute | solution.py:306
  127.1 42.1 %collective-permute-start.26 = (bf16[512,1024]{1,0:T(8,128)(2,1)S(1)}, bf16[512,1024]{1,0:T(8,128)(2,1)S(1)}, u32[]{:S(2)}, u32[]{:S(2)}) collective-permute-start(bf16[512,1024]{1,0:T(8,128)(2,1)S(1)} %collective-permute-done.13.refs_1_.refs_3_), channel_id=1, source_target_pairs={{0,2},{2,0},{4,6},{6,4},{8,10},{10,8},{12,14},{14,12},{16,18},{18,... | collective-permute-start | bytes 3145736 | tf_op jit(solution)/shard_map/ppermute | solution.py:310
  140.3 13.0 %collective-permute-start.19 = (bf16[256,1024]{1,0:T(8,128)(2,1)S(1)}, bf16[256,1024]{1,0:T(8,128)(2,1)S(1)}, u32[]{:S(2)}, u32[]{:S(2)}) collective-permute-start(bf16[256,1024]{1,0:T(8,128)(2,1)S(1)} %constant_dynamic-slice_fusion.5), channel_id=1, source_target_pairs={{0,8},{8,16},{16,24},{24,28},{28,20},{20,12},{12,4},{4,0},{2,6},{1... | collective-permute-start | bytes 1572872 | tf_op jit(solution)/shard_map/ppermute | solution.py:306
  153.9 15.4 %collective-permute-start.27 = (bf16[512,1024]{1,0:T(8,128)(2,1)S(1)}, bf16[512,1024]{1,0:T(8,128)(2,1)S(1)}, u32[]{:S(2)}, u32[]{:S(2)}) collective-permute-start(bf16[512,1024]{1,0:T(8,128)(2,1)S(1)} %collective-permute-done.14.refs_1_.refs_5_), channel_id=1, source_target_pairs={{0,2},{2,0},{4,6},{6,4},{8,10},{10,8},{12,14},{14,12},{16,18},{18,... | collective-permute-start | bytes 3145736 | tf_op jit(solution)/shard_map/ppermute | solution.py:310
  159.7 58.1 %collective-permute-start.16 = (bf16[512,1024]{1,0:T(8,128)(2,1)}, bf16[512,1024]{1,0:T(8,128)(2,1)}, u32[]{:S(2)}, u32[]{:S(2)}) collective-permute-start(bf16[512,1024]{1,0:T(8,128)(2,1)} %convolution_convert_fusion.1), channel_id=1, source_target_pairs={{0,2},{2,0},{4,6},{6,4},{8,10},{10,8},{12,14},{14,12},{16,18},{18,... | collective-permute-start | bytes 3145736 | tf_op jit(solution)/shard_map/ppermute | solution.py:310
  164.5 75.9 %collective-permute-start.15 = (bf16[512,1024]{1,0:T(8,128)(2,1)}, bf16[512,1024]{1,0:T(8,128)(2,1)}, u32[]{:S(2)}, u32[]{:S(2)}) collective-permute-start(bf16[512,1024]{1,0:T(8,128)(2,1)} %convolution_convert_fusion.2), channel_id=1, source_target_pairs={{0,2},{2,0},{4,6},{6,4},{8,10},{10,8},{12,14},{14,12},{16,18},{18,... | collective-permute-start | bytes 3145736 | tf_op jit(solution)/shard_map/ppermute | solution.py:310
  167.3 50.5 %collective-permute-start.21 = (bf16[512,1024]{1,0:T(8,128)(2,1)}, bf16[512,1024]{1,0:T(8,128)(2,1)}, u32[]{:S(2)}, u32[]{:S(2)}) collective-permute-start(bf16[512,1024]{1,0:T(8,128)(2,1)} %add_convert_fusion.5), channel_id=1, source_target_pairs={{0,8},{8,16},{16,24},{24,28},{28,20},{20,12},{12,4},{4,0},{2,6},{1... | collective-permute-start | bytes 3145736 | tf_op jit(solution)/shard_map/ppermute | solution.py:306
  188.9 12.2 %collective-permute-start.35 = (bf16[512,256]{1,0:T(8,128)(2,1)S(1)}, bf16[512,256]{1,0:T(8,128)(2,1)S(1)}, u32[]{:S(2)}, u32[]{:S(2)}) collective-permute-start(bf16[512,256]{1,0:T(8,128)(2,1)S(1)} %dynamic-slice_convert_fusion.3), channel_id=1, source_target_pairs={{0,1},{1,0},{2,3},{3,2},{4,5},{5,4},{6,7},{7,6},{8,9},{9,8},{10,11... | collective-permute-start | bytes 786440 | tf_op jit(solution)/shard_map/ppermute | solution.py:314
  207.4 14.9 %collective-permute-start.36 = (bf16[320,1024]{1,0:T(8,128)(2,1)}, bf16[320,1024]{1,0:T(8,128)(2,1)}, u32[]{:S(2)}, u32[]{:S(2)}) collective-permute-start(bf16[320,1024]{1,0:T(8,128)(2,1)} %maximum_maximum_fusion), channel_id=1, source_target_pairs={{0,2},{2,0},{4,6},{6,4},{8,10},{10,8},{12,14},{14,12},{16,18},{18,... | collective-permute-start | bytes 1966088 | tf_op jit(solution)/shard_map/ppermute | solution.py:310
  220.6 18.1 %collective-permute-start.22 = (bf16[512,1024]{1,0:T(8,128)(2,1)S(1)}, bf16[512,1024]{1,0:T(8,128)(2,1)S(1)}, u32[]{:S(2)}, u32[]{:S(2)}) collective-permute-start(bf16[512,1024]{1,0:T(8,128)(2,1)S(1)} %add_convert_fusion.4), channel_id=1, source_target_pairs={{0,8},{8,16},{16,24},{24,28},{28,20},{20,12},{12,4},{4,0},{2,6},{1... | collective-permute-start | bytes 3145736 | tf_op jit(solution)/shard_map/ppermute | solution.py:306
  238.7 29.2 %collective-permute-start.37 = (bf16[640,1024]{1,0:T(8,128)(2,1)S(1)}, bf16[640,1024]{1,0:T(8,128)(2,1)}, u32[]{:S(2)}, u32[]{:S(2)}) collective-permute-start(bf16[640,1024]{1,0:T(8,128)(2,1)S(1)} %maximum_select_fusion.blob), channel_id=1, source_target_pairs={{0,8},{8,16},{16,24},{24,28},{28,20},{20,12},{12,4},{4,0},{2,6},{1... | collective-permute-start | bytes 3932168 | tf_op jit(solution)/shard_map/ppermute | solution.py:306
  243.7 24.1 %collective-permute-start.23 = (bf16[512,1024]{1,0:T(8,128)(2,1)}, bf16[512,1024]{1,0:T(8,128)(2,1)}, u32[]{:S(2)}, u32[]{:S(2)}) collective-permute-start(bf16[512,1024]{1,0:T(8,128)(2,1)} %add_convert_fusion.3), channel_id=1, source_target_pairs={{0,8},{8,16},{16,24},{24,28},{28,20},{20,12},{12,4},{4,0},{2,6},{1... | collective-permute-start | bytes 3145736 | tf_op jit(solution)/shard_map/ppermute | solution.py:306
  266.3 26.9 %collective-permute-start.48 = (bf16[32,384]{1,0:T(8,128)(2,1)S(1)}, bf16[32,384]{1,0:T(8,128)(2,1)S(1)}, u32[]{:S(2)}, u32[]{:S(2)}) collective-permute-start(bf16[32,384]{1,0:T(8,128)(2,1)S(1)} %convert_element_type.299), channel_id=1, source_target_pairs={{0,1},{1,0},{2,3},{3,2},{4,5},{5,4},{6,7},{7,6},{8,9},{9,8},{10,11... | collective-permute-start | bytes 73736 | tf_op jit(solution)/shard_map/ppermute | solution.py:314
  267.9 17.9 %collective-permute-start.38 = (bf16[640,1024]{1,0:T(8,128)(2,1)}, bf16[640,1024]{1,0:T(8,128)(2,1)}, u32[]{:S(2)}, u32[]{:S(2)}) collective-permute-start(bf16[640,1024]{1,0:T(8,128)(2,1)} %collective-permute-done.37.blob), channel_id=1, source_target_pairs={{0,8},{8,16},{16,24},{24,28},{28,20},{20,12},{12,4},{4,0},{2,6},{1... | collective-permute-start | bytes 3932168 | tf_op jit(solution)/shard_map/ppermute | solution.py:306
  285.8 18.0 %collective-permute-start.39 = (bf16[640,1024]{1,0:T(8,128)(2,1)}, bf16[640,1024]{1,0:T(8,128)(2,1)S(1)}, u32[]{:S(2)}, u32[]{:S(2)}) collective-permute-start(bf16[640,1024]{1,0:T(8,128)(2,1)} %collective-permute-done.38.blob), channel_id=1, source_target_pairs={{0,8},{8,16},{16,24},{24,28},{28,20},{20,12},{12,4},{4,0},{2,6},{1... | collective-permute-start | bytes 3932168 | tf_op jit(solution)/shard_map/ppermute | solution.py:306
  292.6 18.7 %collective-permute-start.31 = (bf16[512,1024]{1,0:T(8,128)(2,1)}, bf16[512,1024]{1,0:T(8,128)(2,1)}, u32[]{:S(2)}, u32[]{:S(2)}) collective-permute-start(bf16[512,1024]{1,0:T(8,128)(2,1)} %convolution_convert_fusion.3), channel_id=1, source_target_pairs={{0,2},{2,0},{4,6},{6,4},{8,10},{10,8},{12,14},{14,12},{16,18},{18,... | collective-permute-start | bytes 3145736 | tf_op jit(solution)/shard_map/ppermute | solution.py:310
  293.2 49.9 %collective-permute-start.30 = (bf16[512,1024]{1,0:T(8,128)(2,1)}, bf16[512,1024]{1,0:T(8,128)(2,1)}, u32[]{:S(2)}, u32[]{:S(2)}) collective-permute-start(bf16[512,1024]{1,0:T(8,128)(2,1)} %convolution_convert_fusion.4), channel_id=1, source_target_pairs={{0,2},{2,0},{4,6},{6,4},{8,10},{10,8},{12,14},{14,12},{16,18},{18,... | collective-permute-start | bytes 3145736 | tf_op jit(solution)/shard_map/ppermute | solution.py:310
  306.3 14.1 %collective-permute-start.41 = (bf16[320,1024]{1,0:T(8,128)(2,1)}, bf16[320,1024]{1,0:T(8,128)(2,1)}, u32[]{:S(2)}, u32[]{:S(2)}) collective-permute-start(bf16[320,1024]{1,0:T(8,128)(2,1)} %constant_dynamic-slice_fusion.4), channel_id=1, source_target_pairs={{0,8},{8,16},{16,24},{24,28},{28,20},{20,12},{12,4},{4,0},{2,6},{1... | collective-permute-start | bytes 1966088 | tf_op jit(solution)/shard_map/ppermute | solution.py:306
  311.2 12.9 %collective-permute-start.49 = (bf16[288,384]{1,0:T(8,128)(2,1)S(1)}, bf16[288,384]{1,0:T(8,128)(2,1)S(1)}, u32[]{:S(2)}, u32[]{:S(2)}) collective-permute-start(bf16[288,384]{1,0:T(8,128)(2,1)S(1)} %pad_maximum_fusion.9), channel_id=1, source_target_pairs={{0,2},{2,0},{4,6},{6,4},{8,10},{10,8},{12,14},{14,12},{16,18},{18,... | collective-permute-start | bytes 663560 | tf_op jit(solution)/shard_map/ppermute | solution.py:310
  320.4 22.7 %collective-permute-start.42 = (bf16[512,1024]{1,0:T(8,128)(2,1)}, bf16[512,1024]{1,0:T(8,128)(2,1)}, u32[]{:S(2)}, u32[]{:S(2)}) collective-permute-start(bf16[512,1024]{1,0:T(8,128)(2,1)} %add_convert_fusion.2), channel_id=1, source_target_pairs={{0,8},{8,16},{16,24},{24,28},{28,20},{20,12},{12,4},{4,0},{2,6},{1... | collective-permute-start | bytes 3145736 | tf_op jit(solution)/shard_map/ppermute | solution.py:306
  324.3 15.9 %collective-permute-start.50 = (bf16[576,384]{1,0:T(8,128)(2,1)S(1)}, bf16[576,384]{1,0:T(8,128)(2,1)S(1)}, u32[]{:S(2)}, u32[]{:S(2)}) collective-permute-start(bf16[576,384]{1,0:T(8,128)(2,1)S(1)} %maximum_select_fusion.3.refs_0_), channel_id=1, source_target_pairs={{0,8},{8,16},{16,24},{24,28},{28,20},{20,12},{12,4},{4,0},{2,6},{1... | collective-permute-start | bytes 1327112 | tf_op jit(solution)/shard_map/ppermute | solution.py:306
  328.5 29.0 %collective-permute-start.29 = (bf16[512,1024]{1,0:T(8,128)(2,1)}, bf16[512,1024]{1,0:T(8,128)(2,1)}, u32[]{:S(2)}, u32[]{:S(2)}) collective-permute-start(bf16[512,1024]{1,0:T(8,128)(2,1)} %convolution_convert_fusion.5), channel_id=1, source_target_pairs={{0,2},{2,0},{4,6},{6,4},{8,10},{10,8},{12,14},{14,12},{16,18},{18,... | collective-permute-start | bytes 3145736 | tf_op jit(solution)/shard_map/ppermute | solution.py:310
  341.5 12.4 %collective-permute-start.51 = (bf16[576,384]{1,0:T(8,128)(2,1)S(1)}, bf16[576,384]{1,0:T(8,128)(2,1)S(1)}, u32[]{:S(2)}, u32[]{:S(2)}) collective-permute-start(bf16[576,384]{1,0:T(8,128)(2,1)S(1)} %collective-permute-done.50.refs_1_), channel_id=1, source_target_pairs={{0,2},{2,0},{4,6},{6,4},{8,10},{10,8},{12,14},{14,12},{16,18},{18,... | collective-permute-start | bytes 1327112 | tf_op jit(solution)/shard_map/ppermute | solution.py:310
  341.5 11.8 %collective-permute-start.52 = (bf16[576,384]{1,0:T(8,128)(2,1)S(1)}, bf16[576,384]{1,0:T(8,128)(2,1)S(1)}, u32[]{:S(2)}, u32[]{:S(2)}) collective-permute-start(bf16[576,384]{1,0:T(8,128)(2,1)S(1)} %collective-permute-done.50.refs_1_), channel_id=1, source_target_pairs={{0,8},{8,16},{16,24},{24,28},{28,20},{20,12},{12,4},{4,0},{2,6},{1... | collective-permute-start | bytes 1327112 | tf_op jit(solution)/shard_map/ppermute | solution.py:306
  345.8 15.3 %collective-permute-start.43 = (bf16[512,1024]{1,0:T(8,128)(2,1)S(1)}, bf16[512,1024]{1,0:T(8,128)(2,1)S(1)}, u32[]{:S(2)}, u32[]{:S(2)}) collective-permute-start(bf16[512,1024]{1,0:T(8,128)(2,1)S(1)} %add_convert_fusion.1), channel_id=1, source_target_pairs={{0,8},{8,16},{16,24},{24,28},{28,20},{20,12},{12,4},{4,0},{2,6},{1... | collective-permute-start | bytes 3145736 | tf_op jit(solution)/shard_map/ppermute | solution.py:306
  350.3 65.7 %collective-permute-start.61 = (bf16[640,1024]{1,0:T(8,128)(2,1)}, bf16[640,1024]{1,0:T(8,128)(2,1)S(1)}, u32[]{:S(2)}, u32[]{:S(2)}) collective-permute-start(bf16[640,1024]{1,0:T(8,128)(2,1)} %collective-permute-done.37.blob), channel_id=1, source_target_pairs={{0,2},{2,0},{4,6},{6,4},{8,10},{10,8},{12,14},{14,12},{16,18},{18,... | collective-permute-start | bytes 3932168 | tf_op jit(solution)/shard_map/ppermute | solution.py:310
  364.3 28.7 %collective-permute-start.44 = (bf16[512,1024]{1,0:T(8,128)(2,1)}, bf16[512,1024]{1,0:T(8,128)(2,1)}, u32[]{:S(2)}, u32[]{:S(2)}) collective-permute-start(bf16[512,1024]{1,0:T(8,128)(2,1)} %add_convert_fusion), channel_id=1, source_target_pairs={{0,8},{8,16},{16,24},{24,28},{28,20},{20,12},{12,4},{4,0},{2,6},{1... | collective-permute-start | bytes 3145736 | tf_op jit(solution)/shard_map/ppermute | solution.py:306
  367.3 14.4 %collective-permute-start.56 = (bf16[288,384]{1,0:T(8,128)(2,1)S(1)}, bf16[288,384]{1,0:T(8,128)(2,1)S(1)}, u32[]{:S(2)}, u32[]{:S(2)}) collective-permute-start(bf16[288,384]{1,0:T(8,128)(2,1)S(1)} %constant_dynamic-slice_fusion), channel_id=1, source_target_pairs={{0,8},{8,16},{16,24},{24,28},{28,20},{20,12},{12,4},{4,0},{2,6},{1... | collective-permute-start | bytes 663560 | tf_op jit(solution)/shard_map/ppermute | solution.py:306
  369.1 13.9 %collective-permute-start.55 = (bf16[576,384]{1,0:T(8,128)(2,1)S(1)}, bf16[576,384]{1,0:T(8,128)(2,1)S(1)}, u32[]{:S(2)}, u32[]{:S(2)}) collective-permute-start(bf16[576,384]{1,0:T(8,128)(2,1)S(1)} %collective-permute-done.54.refs_5_), channel_id=1, source_target_pairs={{0,2},{2,0},{4,6},{6,4},{8,10},{10,8},{12,14},{14,12},{16,18},{18,... | collective-permute-start | bytes 1327112 | tf_op jit(solution)/shard_map/ppermute | solution.py:310
  382.5 38.9 %collective-permute-start.60 = (bf16[640,1024]{1,0:T(8,128)(2,1)}, bf16[640,1024]{1,0:T(8,128)(2,1)}, u32[]{:S(2)}, u32[]{:S(2)}) collective-permute-start(bf16[640,1024]{1,0:T(8,128)(2,1)} %collective-permute-done.38.blob), channel_id=1, source_target_pairs={{0,2},{2,0},{4,6},{6,4},{8,10},{10,8},{12,14},{14,12},{16,18},{18,... | collective-permute-start | bytes 3932168 | tf_op jit(solution)/shard_map/ppermute | solution.py:310
  383.0 43.1 %collective-permute-start.59 = (bf16[640,1024]{1,0:T(8,128)(2,1)S(1)}, bf16[640,1024]{1,0:T(8,128)(2,1)}, u32[]{:S(2)}, u32[]{:S(2)}) collective-permute-start(bf16[640,1024]{1,0:T(8,128)(2,1)S(1)} %collective-permute-done.39.blob), channel_id=1, source_target_pairs={{0,2},{2,0},{4,6},{6,4},{8,10},{10,8},{12,14},{14,12},{16,18},{18,... | collective-permute-start | bytes 3932168 | tf_op jit(solution)/shard_map/ppermute | solution.py:310
  392.4 36.4 %collective-permute-start.58 = (bf16[320,1024]{1,0:T(8,128)(2,1)}, bf16[320,1024]{1,0:T(8,128)(2,1)}, u32[]{:S(2)}, u32[]{:S(2)}) collective-permute-start(bf16[320,1024]{1,0:T(8,128)(2,1)} %collective-permute-done.41), channel_id=1, source_target_pairs={{0,2},{2,0},{4,6},{6,4},{8,10},{10,8},{12,14},{14,12},{16,18},{18,... | collective-permute-start | bytes 1966088 | tf_op jit(solution)/shard_map/ppermute | solution.py:310
  396.5 35.8 %collective-permute-start.45 = (bf16[256,1024]{1,0:T(8,128)(2,1)}, bf16[256,1024]{1,0:T(8,128)(2,1)}, u32[]{:S(2)}, u32[]{:S(2)}) collective-permute-start(bf16[256,1024]{1,0:T(8,128)(2,1)} %dynamic-slice_convert_fusion), channel_id=1, source_target_pairs={{0,2},{2,0},{4,6},{6,4},{8,10},{10,8},{12,14},{14,12},{16,18},{18,... | collective-permute-start | bytes 1572872 | tf_op jit(solution)/shard_map/ppermute | solution.py:310
  416.0 17.9 %collective-permute-start.24 = (bf16[256,1024]{1,0:T(8,128)(2,1)S(1)}, bf16[256,1024]{1,0:T(8,128)(2,1)S(1)}, u32[]{:S(2)}, u32[]{:S(2)}) collective-permute-start(bf16[256,1024]{1,0:T(8,128)(2,1)S(1)} %copy-done.74), channel_id=1, source_target_pairs={{0,2},{2,0},{4,6},{6,4},{8,10},{10,8},{12,14},{14,12},{16,18},{18,... | collective-permute-start | bytes 1572872 | tf_op jit(solution)/shard_map/ppermute | solution.py:310
  (118 other events, 1114.8 us)
